TPU v7x, 32 devices: a whole 2x2x4 slice. The times are simulated.
32 devices in a mesh: table: 32 (over z, y, x, core), dp: 1.
Axes of the slice: x: 2, y: 2, z: 4, core: 2. Of those that a mesh axis runs over, the one named last changes fastest.
Arguments:
- table: bfloat16 [12288, 512], P('table'), may hold values from -6 to 6
- owner: int32 [32, 256, 1], P(('table', 'dp')), may hold values from 0 to 31; in each aligned block of 256 rows (0 to 255, 256 to 511, ..., all dimensions but the last counted through in order) at most 16 rows name the same one
- row_in_shard: int32 [32, 256], P(('table', 'dp')), may hold values from 0 to 383
- segment: int32 [32, 256], P(('table', 'dp')), may hold values from 0 to 3, never falling along the last dimension, each value on 1 to 128 neighbouring positions
- w_in: bfloat16 [512, 2048], replicated, may hold values from -0.25 to 0.25
- w_out: bfloat16 [512, 512], replicated, may hold values from -0.25 to 0.25
- cotangent: bfloat16 [32, 256, 512], P(('table', 'dp')), may hold values from -6 to 6
Outputs:
- layer_out: bfloat16 [32, 256, 512], P(('table', 'dp'))
- grad_table: float32 [12288, 512], P('table')
- grad_w_in: float32 [512, 2048], P(None, 'dp')
- grad_w_out: float32 [512, 512], P('dp')
Inputs may be any that keep to these rules, and one draw needn't show every extreme that they name: `owner`: among one device's 256 positions no shard is named more than 16 times, a bound that some block reaches. `segment`: never falls along a buffer; each history has 1 to 128 positions and one has exactly 128.
All inputs are finite; a program needn't handle non-finite values.
Results may differ from a plain program's by a relative error of at most 0.019.
Values may be sent and summed in bfloat16 or wider, within the bound.
A program may use at most 64 MiB of HBM per device.

v0:
```python
import jax
import jax.numpy as jnp
from jax import lax
from jax.sharding import PartitionSpec as P

HEADS = 8


EPS = 1e-05


def normalize(values):
    average = jnp.mean(values, axis=-1, keepdims=True)
    centred = values - average
    spread = jnp.mean(centred * centred, axis=-1, keepdims=True)
    return centred * lax.rsqrt(spread + EPS)


def hstu_layer(embedded, w_in, w_out, segment):
    row_count, width = embedded.shape
    head_size = width // HEADS
    normed = normalize(embedded.astype(jnp.float32)).astype(jnp.bfloat16)
    mixed_all = jax.nn.silu(jnp.dot(normed, w_in, preferred_element_type=jnp.float32)).astype(
        jnp.bfloat16
    )
    gate_part = mixed_all[:, :width]
    value_part = mixed_all[:, width : 2 * width].reshape(row_count, HEADS, head_size)
    query_part = mixed_all[:, 2 * width : 3 * width].reshape(row_count, HEADS, head_size)
    key_part = mixed_all[:, 3 * width :].reshape(row_count, HEADS, head_size)
    position = jnp.arange(row_count)
    allowed = (segment[:, None] == segment[None, :]) & (position[None, :] <= position[:, None])
    scores = jnp.einsum(
        "qhd,khd->hqk", query_part, key_part, preferred_element_type=jnp.float32
    ) * head_size ** (-0.5)
    weights = jnp.where(allowed[None], jax.nn.silu(scores), 0.0).astype(jnp.bfloat16)
    attended = jnp.einsum(
        "hqk,khd->qhd", weights, value_part, preferred_element_type=jnp.float32
    ).reshape(row_count, width)
    gated = (normalize(attended) * gate_part.astype(jnp.float32)).astype(jnp.bfloat16)
    result = embedded.astype(jnp.float32) + jnp.dot(
        gated, w_out, preferred_element_type=jnp.float32
    )
    return result.astype(jnp.bfloat16)


def on_device(table, owner, row_in_shard, segment, w_in, w_out, cotangent):
    shards = lax.axis_size("table")
    row_count = owner.shape[1]
    capacity = 2 * row_count // shards
    slot_total = shards * capacity
    vocab_rows = table.shape[0]
    target = owner[0, :, 0]
    local_row = row_in_shard[0]
    chosen = target[:, None] == jnp.arange(shards)[None, :]
    rank_all = jnp.cumsum(chosen.astype(jnp.int32), axis=0) - 1
    rank_own = jnp.sum(jnp.where(chosen, rank_all, 0), axis=1)
    slot_index = target * capacity + rank_own
    slot_match = slot_index[None, :] == jnp.arange(slot_total)[:, None]
    filled = jnp.any(slot_match, axis=1)
    source_row = jnp.sum(jnp.where(slot_match, jnp.arange(row_count)[None, :], 0), axis=1)
    request = jnp.where(filled, jnp.take(local_row, source_row), -1).reshape(shards, capacity)
    asked_rows = lax.all_to_all(request, "table", split_axis=0, concat_axis=0, tiled=True)
    is_valid = asked_rows >= 0
    found_rows = jnp.take(table, jnp.maximum(asked_rows, 0).reshape(-1), axis=0).reshape(
        shards, capacity, -1
    )
    found_rows = jnp.where(is_valid[..., None], found_rows, jnp.zeros((), table.dtype))
    returned = lax.all_to_all(found_rows, "table", split_axis=0, concat_axis=0, tiled=True)
    embedded = jnp.take(returned.reshape(slot_total, -1), slot_index, axis=0)
    seg_rows = segment[0]

    def local_layer(emb_in, weight_in, weight_out):
        return hstu_layer(emb_in, weight_in, weight_out, seg_rows)

    layer_rows, pullback = jax.vjp(local_layer, embedded, w_in, w_out)
    d_emb, d_in, d_out = pullback(cotangent[0])
    sent_grads = jnp.where(
        filled[:, None], jnp.take(d_emb, source_row, axis=0), jnp.zeros((), d_emb.dtype)
    )
    arrived = lax.all_to_all(
        sent_grads.reshape(shards, capacity, -1), "table", split_axis=0, concat_axis=0, tiled=True
    )
    flat_grads = arrived.reshape(slot_total, -1)
    table_ids = jnp.where(is_valid, asked_rows, vocab_rows).reshape(-1)
    partial_sum = jax.ops.segment_sum(
        flat_grads.astype(jnp.float32), table_ids, num_segments=vocab_rows + 1
    )[:vocab_rows]
    grad_table = lax.psum(partial_sum.astype(jnp.bfloat16), "dp").astype(jnp.float32)
    share_in, share_out = (
        lax.psum_scatter(
            d_in.astype(jnp.float32).astype(jnp.bfloat16), "dp", scatter_dimension=1, tiled=True
        ).astype(jnp.float32),
        lax.psum_scatter(
            d_out.astype(jnp.float32).astype(jnp.bfloat16), "dp", scatter_dimension=0, tiled=True
        ).astype(jnp.float32),
    )
    grad_w_in, grad_w_out = lax.psum((share_in, share_out), "table")
    return (layer_rows[None], grad_table, grad_w_in, grad_w_out)


def solution(mesh):
    placed = (
        P("table", None),
        P(("table", "dp"), None, None),
        P(("table", "dp"), None),
        P(("table", "dp"), None),
        P(),
        P(),
        P(("table", "dp"), None, None),
    )
    return jax.shard_map(
        on_device,
        mesh=mesh,
        in_specs=placed,
        out_specs=(P(("table", "dp"), None, None), P("table", None), P(None, "dp"), P("dp", None)),
        check_vma=False,
    )
```

profile of v0, /device:TPU:0, one launch (start us, length us, event | category | flops | bytes accessed | tf_op | source)
XLA Modules:
  0.0 250.4 jit_solution(2802016858434944229)
XLA Ops:
  10.8 3.6 %gather_fusion = s32[512]{0:T(512)S(1)} fusion(s32[256]{0:T(256)} %bitcast.92, s32[1024]{0:T(1024)S(1)} %pad_clamp_fusion.2), kind=kCustom, calls=%fused_computation | custom fusion | bytes 6144 | tf_op jit(solution)/shard_map/jit(_take)/gather | solution.py:61
  14.5 14.3 %all_to_all.19 = s32[32,1,16]{2,1,0:T(1,128)S(1)} all-to-all(s32[32,1,16]{2,1,0:T(1,128)S(1)} %bitcast.110), channel_id=1, replica_groups=mesh['table'=32,'dp'=1] {'table'}, dimensions={0} | all-to-all | bytes 4096 | tf_op jit(solution)/shard_map/all_to_all | solution.py:62
  30.1 2.0 gather_fusion.1
  33.1 2.6 %all-to-all-start.1 = ((bf16[32,16,512]{2,1,0:T(8,128)(2,1)}), bf16[32,16,512]{2,1,0:T(8,128)(2,1)S(1)}, u32[]{:S(2)}, u32[]{:S(2)}) async-start(bf16[32,16,512]{2,1,0:T(8,128)(2,1)} %select_select_fusion.1), calls=%async_computation.1 | async-start | bytes 1048576 | tf_op jit(solution)/shard_map/all_to_all | solution.py:68
  36.3 15.0 %all-to-all-done.1 = bf16[32,16,512]{2,1,0:T(8,128)(2,1)S(1)} async-done(((bf16[32,16,512]{2,1,0:T(8,128)(2,1)}), bf16[32,16,512]{2,1,0:T(8,128)(2,1)S(1)}, u32[]{:S(2)}, u32[]{:S(2)}) %all-to-all-start.1) | async-done | bytes 524320 | tf_op jit(solution)/shard_map/all_to_all | solution.py:68
  51.3 1.2 gather_fusion.2
  52.9 2.2 multiply_convert_fusion
  56.6 2.1 select_convert_fusion
  59.9 1.6 multiply_reduce_fusion
  61.5 2.0 fusion.42
  63.8 2.3 fusion.45
  66.1 3.0 %fusion.5 = bf16[8,256,256]{2,1,0:T(8,128)(2,1)S(1)} fusion(f32[8,256,256]{2,1,0:T(8,128)} %get-tuple-element.24, bf16[8,64,256]{2,1,0:T(8,128)(2,1)} %bitcast.107, bf16[256,8,64]{0,2,1:T(8,128)(2,1)S(1)} %bitcast.99, pred[256,256]{1,0:T(8,128)(4,1)S(1)} %fusion.29), kind=kOutput, calls=%fused_computation.15 | convolution fusion | flops 74448896 | bytes 3735552 | tf_op jit(solution)/shard_map/transpose(jvp(hqk,khd->qhd))/dot_general | solution.py:36
  72.1 1.8 copy.52
  74.8 1.3 fusion.6
  76.1 5.1 %fusion = f32[512,2048]{1,0:T(8,128)} fusion(f32[256]{0:T(256)S(1)} %fusion.34, f32[256]{0:T(256)S(1)} %broadcast_multiply_fusion.1, bf16[256,512]{1,0:T(8,128)(2,1)S(1)} %gather_fusion.2, pred[256]{0:T(512)(128)(4,1)S(1)} %get-tuple-element.8, f32[256,2048]{1,0:T(8,128)} %get-tuple-element.22, bf16[256,512]{1,0:T(8,128)(2,1)S(1)} %copy-done.15, ...), kind=kOutput, calls=%fused_computation.8 | convolution fusion | flops 548536320 | bytes 7604480 | tf_op jit(solution)/shard_map/transpose(jvp())/dot_general | solution.py:23
  82.1 3.3 %fusion.20 = (f32[256]{0:T(256)S(1)}, f32[256,512]{1,0:T(8,128)S(1)}) fusion(f32[256]{0:T(256)S(1)} %broadcast_multiply_fusion.1, bf16[256,512]{1,0:T(8,128)(2,1)S(1)} %gather_fusion.2, pred[256]{0:T(512)(128)(4,1)S(1)} %get-tuple-element.8, bf16[512,2048]{1,0:T(8,128)(2,1)S(1)} %copy-done, f32[256,2048]{1,0:T(8,128)} %get-tuple-element.22, ...), kind=kOutput, calls=%fused_computation.49 | convolution fusion | flops 546701056 | bytes 6031616 | tf_op jit(solution)/shard_map/transpose(jvp())/dot_general | solution.py:23
  86.0 2.0 gather_fusion.3
  89.0 3.2 %all-to-all-start.2 = ((bf16[32,16,512]{2,1,0:T(8,128)(2,1)}), bf16[32,16,512]{2,1,0:T(8,128)(2,1)S(1)}, u32[]{:S(2)}, u32[]{:S(2)}) async-start(bf16[32,16,512]{2,1,0:T(8,128)(2,1)} %select_select_fusion), calls=%async_computation.2 | async-start | bytes 1048576 | tf_op jit(solution)/shard_map/all_to_all | solution.py:80
  92.2 2.1 fusion.10
  94.2 18.9 %all-to-all-done.2 = bf16[32,16,512]{2,1,0:T(8,128)(2,1)S(1)} async-done(((bf16[32,16,512]{2,1,0:T(8,128)(2,1)}), bf16[32,16,512]{2,1,0:T(8,128)(2,1)S(1)}, u32[]{:S(2)}, u32[]{:S(2)}) %all-to-all-start.2) | async-done | bytes 524320 | tf_op jit(solution)/shard_map/all_to_all | solution.py:80
  113.2 4.6 %scatter_custom_fusion = f32[385,512]{1,0:T(8,128)} fusion(s32[512]{0:T(512)S(1)} %bitcast.120, bf16[512,512]{1,0:T(8,128)(2,1)S(1)} %bitcast.95, f32[]{:T(128)} %constant.95.clone.1), kind=kCustom, calls=%fused_computation.33 | custom fusion | flops 524288 | bytes 1312772 | tf_op jit(solution)/shard_map/scatter-add | solution.py:85
  117.7 2.1 fusion.25
  119.8 118.0 %all-reduce.7.cloned.1.call-done = (f32[512,2048]{1,0:T(8,128)}, f32[512,512]{1,0:T(8,128)}) async-done(((f32[512,2048]{1,0:T(8,128)}, f32[512,512]{1,0:T(8,128)}), (f32[512,2048]{1,0:T(8,128)}, f32[512,512]{1,0:T(8,128)})) %all-reduce.7.cloned.1.call-update) | async-done | bytes 5242896 | tf_op jit(solution)/shard_map/psum | solution.py:97
  237.8 4.8 %copy.59 = f32[512,2048]{1,0:T(8,128)} copy(f32[512,2048]{1,0:T(8,128)} %get-tuple-element.33) | data formatting | bytes 8388608
  (94 shorter events, 17.2 us)
Async XLA Ops:
  7.2 45.7 %copy-start = (bf16[512,2048]{1,0:T(8,128)(2,1)S(1)}, bf16[512,2048]{1,0:T(8,128)(2,1)}, u32[]{:S(2)}) copy-start(bf16[512,2048]{1,0:T(8,128)(2,1)} %param.11) | copy-start | bytes 6291460
  7.2 22.9 %copy-start.1 = (bf16[384,512]{1,0:T(8,128)(2,1)S(1)}, bf16[384,512]{1,0:T(8,128)(2,1)}, u32[]{:S(2)}) copy-start(bf16[384,512]{1,0:T(8,128)(2,1)} %param.7) | copy-start | bytes 1179652
  32.1 4.0 %copy-start.17 = (s32[1,256,1]{1,2,0:T(1,128)S(1)}, s32[1,256,1]{1,2,0:T(1,128)}, u32[]{:S(2)}) copy-start(s32[1,256,1]{1,2,0:T(1,128)} %param.8) | copy-start | bytes 3076
  32.1 4.1 %copy-start.18 = (s32[1,256]{1,0:T(1,128)S(1)}, s32[1,256]{1,0:T(1,128)}, u32[]{:S(2)}) copy-start(s32[1,256]{1,0:T(1,128)} %param.10) | copy-start | bytes 3076
  33.1 18.2 %all-to-all-start.1 = ((bf16[32,16,512]{2,1,0:T(8,128)(2,1)}), bf16[32,16,512]{2,1,0:T(8,128)(2,1)S(1)}, u32[]{:S(2)}, u32[]{:S(2)}) async-start(bf16[32,16,512]{2,1,0:T(8,128)(2,1)} %select_select_fusion.1), calls=%async_computation.1 | async-start | bytes 1048576 | tf_op jit(solution)/shard_map/all_to_all | solution.py:68
  35.7 202.0 %all-reduce.7.cloned.1.call-start = ((), (), s32[]{:S(2)}) async-start(), calls=%async_computation.3 | async-start | bytes 10485760 | tf_op jit(solution)/shard_map/psum | solution.py:97
  55.1 1.0 copy-start.4
  56.2 2.4 copy-start.8
  56.4 2.3 copy-start.10
  56.5 2.1 copy-start.5
  58.7 1.0 copy-start.2
  61.5 4.6 %copy-start.6 = (bf16[256,512]{0,1:T(8,128)(2,1)S(1)}, bf16[256,512]{0,1:T(8,128)(2,1)}, u32[]{:S(2)}) copy-start(bf16[256,512]{0,1:T(8,128)(2,1)} %copy-done.5) | copy-start | bytes 786436
  63.8 2.3 copy-start.14
  66.1 3.0 %copy-start.9 = (bf16[256,512]{0,1:T(8,128)(2,1)S(1)}, bf16[256,512]{0,1:T(8,128)(2,1)}, u32[]{:S(2)}) copy-start(bf16[256,512]{0,1:T(8,128)(2,1)} %copy-done.8) | copy-start | bytes 786436
  66.1 4.2 %copy-start.11 = (bf16[256,512]{0,1:T(8,128)(2,1)S(1)}, bf16[256,512]{0,1:T(8,128)(2,1)}, u32[]{:S(2)}) copy-start(bf16[256,512]{0,1:T(8,128)(2,1)} %copy-done.10) | copy-start | bytes 786436
  69.1 2.2 copy-start.12
  69.1 5.7 %copy-start.3 = (bf16[1,256,512]{2,1,0:T(8,128)(2,1)S(1)}, bf16[1,256,512]{2,1,0:T(8,128)(2,1)}, u32[]{:S(2)}) copy-start(bf16[1,256,512]{2,1,0:T(8,128)(2,1)} %param.13) | copy-start | bytes 786436
  70.3 3.7 %copy-start.13 = (bf16[8,256,64]{1,2,0:T(8,128)(2,1)S(1)}, bf16[8,256,64]{1,2,0:T(8,128)(2,1)}, u32[]{:S(2)}) copy-start(bf16[8,256,64]{1,2,0:T(8,128)(2,1)} %fusion.46) | copy-start | bytes 786436
  72.1 4.0 %copy-start.15 = (bf16[256,512]{1,0:T(8,128)(2,1)S(1)}, bf16[256,512]{1,0:T(8,128)(2,1)}, u32[]{:S(2)}) copy-start(bf16[256,512]{1,0:T(8,128)(2,1)} %get-tuple-element.11) | copy-start | bytes 786436
  81.2 0.9 copy-start.16
  89.0 24.2 %all-to-all-start.2 = ((bf16[32,16,512]{2,1,0:T(8,128)(2,1)}), bf16[32,16,512]{2,1,0:T(8,128)(2,1)S(1)}, u32[]{:S(2)}, u32[]{:S(2)}) async-start(bf16[32,16,512]{2,1,0:T(8,128)(2,1)} %select_select_fusion), calls=%async_computation.2 | async-start | bytes 1048576 | tf_op jit(solution)/shard_map/all_to_all | solution.py:80
  237.8 4.8 %copy-start.7 = (f32[512,512]{1,0:T(8,128)S(1)}, f32[512,512]{1,0:T(8,128)}, u32[]{:S(2)}) copy-start(f32[512,512]{1,0:T(8,128)} %get-tuple-element.34) | copy-start | bytes 3145732
Sparse Core Ops, SparseCore 0:
  81.3 156.4 all-reduce.6
where the time goes:
time: 251 us; the launch traced here: 250 us
  waiting for transfers between devices  152 us (61%)
  matrix products  25.5 us (10%)
  local copies, waits for them, and re-layouts  22.3 us (9%)
  other arithmetic  16 us (6%)
  between operations  14.4 us (6%)
  blocking collectives  14.3 us (6%)
  starting transfers between devices  6.04 us (2%)
    psum x1, waiting for transfers between devices, on_device(): grad_w_in, grad_w_out = lax.psum((share_in, share_out), 'table')  118 us
    all_to_all x1, waiting for transfers between devices, on_device(): lax.all_to_all(sent_grads.reshape(shards, capacity, -1), 'table', split_a...  18.9 us
    all_to_all x1, waiting for transfers between devices, on_device(): lax.all_to_all(found_rows, 'table', split_axis=0, concat_axis=0, tiled=True)  15 us
    all_to_all x1, blocking collectives, on_device(): lax.all_to_all(request, 'table', split_axis=0, concat_axis=0, tiled=True)  14.3 us
    dot_general x3, matrix products, hstu_layer(): jnp.dot(normed, w_in, preferred_element_type=jnp.float32)  10.5 us
    unnamed x40, local copies, waits for them, and re-layouts  8.13 us
    dot_general x3, matrix products, hstu_layer(): jnp.einsum('hqk,khd->qhd', weights, value_part, preferred_element_type=jn...  5.75 us
  transfers between devices with their start and end apart: 3, of which 3 were waited for; matrix products, arithmetic and copies ran while one was open for 6% of the time, Pallas kernels for 0%

commit v1 on v0

--- a/solution.py
+++ b/solution.py
@@ -51,9 +51,9 @@
     vocab_rows = table.shape[0]
     target = owner[0, :, 0]
     local_row = row_in_shard[0]
-    chosen = target[:, None] == jnp.arange(shards)[None, :]
-    rank_all = jnp.cumsum(chosen.astype(jnp.int32), axis=0) - 1
-    rank_own = jnp.sum(jnp.where(chosen, rank_all, 0), axis=1)
+    positions = jnp.arange(row_count)
+    earlier = (target[None, :] == target[:, None]) & (positions[None, :] < positions[:, None])
+    rank_own = jnp.sum(earlier.astype(jnp.int32), axis=1)
     slot_index = target * capacity + rank_own
     slot_match = slot_index[None, :] == jnp.arange(slot_total)[:, None]
     filled = jnp.any(slot_match, axis=1)

time: 251 us -> 250 us (level)
  no operation moved by 1% of the time
where the time goes in v1:
time: 250 us; the launch traced here: 249 us
  waiting for transfers between devices  152 us (61%)
  matrix products  25.5 us (10%)
  local copies, waits for them, and re-layouts  22.1 us (9%)
  other arithmetic  14.8 us (6%)
  between operations  14.4 us (6%)
  blocking collectives  14.3 us (6%)
  starting transfers between devices  6 us (2%)
    psum x1, waiting for transfers between devices, on_device(): grad_w_in, grad_w_out = lax.psum((share_in, share_out), 'table')  118 us
    all_to_all x1, waiting for transfers between devices, on_device(): lax.all_to_all(sent_grads.reshape(shards, capacity, -1), 'table', split_a...  18.9 us
    all_to_all x1, waiting for transfers between devices, on_device(): lax.all_to_all(found_rows, 'table', split_axis=0, concat_axis=0, tiled=True)  15 us
    all_to_all x1, blocking collectives, on_device(): lax.all_to_all(request, 'table', split_axis=0, concat_axis=0, tiled=True)  14.3 us
    dot_general x3, matrix products, hstu_layer(): jnp.dot(normed, w_in, preferred_element_type=jnp.float32)  10.5 us
    unnamed x40, local copies, waits for them, and re-layouts  8.13 us
    dot_general x3, matrix products, hstu_layer(): jnp.einsum('hqk,khd->qhd', weights, value_part, preferred_element_type=jn...  5.75 us
  transfers between devices with their start and end apart: 3, of which 3 were waited for; matrix products, arithmetic and copies ran while one was open for 6% of the time, Pallas kernels for 0%

profile of v1, /device:TPU:0, one launch (start us, length us, event | category | flops | bytes accessed | tf_op | source)
XLA Modules:
  0.0 248.9 jit_solution(9092655413568203071)
XLA Ops:
  9.4 3.6 %gather_fusion = s32[512]{0:T(512)S(1)} fusion(s32[256]{0:T(256)} %bitcast.76, s32[1024]{0:T(1024)S(1)} %pad_clamp_fusion.2), kind=kCustom, calls=%fused_computation | custom fusion | bytes 6144 | tf_op jit(solution)/shard_map/jit(_take)/gather | solution.py:61
  13.1 14.3 %all_to_all.19 = s32[32,1,16]{2,1,0:T(1,128)S(1)} all-to-all(s32[32,1,16]{2,1,0:T(1,128)S(1)} %bitcast.94), channel_id=1, replica_groups=mesh['table'=32,'dp'=1] {'table'}, dimensions={0} | all-to-all | bytes 4096 | tf_op jit(solution)/shard_map/all_to_all | solution.py:62
  28.7 2.0 gather_fusion.1
  31.7 2.6 %all-to-all-start.1 = ((bf16[32,16,512]{2,1,0:T(8,128)(2,1)}), bf16[32,16,512]{2,1,0:T(8,128)(2,1)S(1)}, u32[]{:S(2)}, u32[]{:S(2)}) async-start(bf16[32,16,512]{2,1,0:T(8,128)(2,1)} %select_select_fusion.1), calls=%async_computation.1 | async-start | bytes 1048576 | tf_op jit(solution)/shard_map/all_to_all | solution.py:68
  34.9 15.0 %all-to-all-done.1 = bf16[32,16,512]{2,1,0:T(8,128)(2,1)S(1)} async-done(((bf16[32,16,512]{2,1,0:T(8,128)(2,1)}), bf16[32,16,512]{2,1,0:T(8,128)(2,1)S(1)}, u32[]{:S(2)}, u32[]{:S(2)}) %all-to-all-start.1) | async-done | bytes 524320 | tf_op jit(solution)/shard_map/all_to_all | solution.py:68
  49.9 1.2 gather_fusion.2
  51.5 2.2 multiply_convert_fusion
  55.2 2.1 select_convert_fusion
  58.5 1.6 multiply_reduce_fusion
  60.1 2.0 fusion.40
  62.4 2.3 fusion.43
  64.7 3.0 %fusion.5 = bf16[8,256,256]{2,1,0:T(8,128)(2,1)S(1)} fusion(f32[8,256,256]{2,1,0:T(8,128)} %get-tuple-element.24, bf16[8,64,256]{2,1,0:T(8,128)(2,1)} %bitcast.91, bf16[256,8,64]{0,2,1:T(8,128)(2,1)S(1)} %bitcast.83, pred[256,256]{1,0:T(8,128)(4,1)S(1)} %fusion.30), kind=kOutput, calls=%fused_computation.15 | convolution fusion | flops 74448896 | bytes 3735552 | tf_op jit(solution)/shard_map/transpose(jvp(hqk,khd->qhd))/dot_general | solution.py:36
  70.7 1.8 copy.49
  73.4 1.3 fusion.6
  74.7 5.1 %fusion = f32[512,2048]{1,0:T(8,128)} fusion(f32[256]{0:T(256)S(1)} %fusion.32, f32[256]{0:T(256)S(1)} %broadcast_multiply_fusion.1, bf16[256,512]{1,0:T(8,128)(2,1)S(1)} %gather_fusion.2, pred[256]{0:T(512)(128)(4,1)S(1)} %get-tuple-element.8, f32[256,2048]{1,0:T(8,128)} %get-tuple-element.22, bf16[256,512]{1,0:T(8,128)(2,1)S(1)} %copy-done.15, ...), kind=kOutput, calls=%fused_computation.8 | convolution fusion | flops 548536320 | bytes 7604480 | tf_op jit(solution)/shard_map/transpose(jvp())/dot_general | solution.py:23
  80.7 3.2 %fusion.20 = (f32[256]{0:T(256)S(1)}, f32[256,512]{1,0:T(8,128)S(1)}) fusion(f32[256]{0:T(256)S(1)} %broadcast_multiply_fusion.1, bf16[256,512]{1,0:T(8,128)(2,1)S(1)} %gather_fusion.2, pred[256]{0:T(512)(128)(4,1)S(1)} %get-tuple-element.8, bf16[512,2048]{1,0:T(8,128)(2,1)S(1)} %copy-done, f32[256,2048]{1,0:T(8,128)} %get-tuple-element.22, ...), kind=kOutput, calls=%fused_computation.49 | convolution fusion | flops 546701056 | bytes 6031616 | tf_op jit(solution)/shard_map/transpose(jvp())/dot_general | solution.py:23
  84.6 2.0 gather_fusion.3
  87.6 3.2 %all-to-all-start.2 = ((bf16[32,16,512]{2,1,0:T(8,128)(2,1)}), bf16[32,16,512]{2,1,0:T(8,128)(2,1)S(1)}, u32[]{:S(2)}, u32[]{:S(2)}) async-start(bf16[32,16,512]{2,1,0:T(8,128)(2,1)} %select_select_fusion), calls=%async_computation.2 | async-start | bytes 1048576 | tf_op jit(solution)/shard_map/all_to_all | solution.py:80
  90.8 2.1 fusion.10
  92.8 18.9 %all-to-all-done.2 = bf16[32,16,512]{2,1,0:T(8,128)(2,1)S(1)} async-done(((bf16[32,16,512]{2,1,0:T(8,128)(2,1)}), bf16[32,16,512]{2,1,0:T(8,128)(2,1)S(1)}, u32[]{:S(2)}, u32[]{:S(2)}) %all-to-all-start.2) | async-done | bytes 524320 | tf_op jit(solution)/shard_map/all_to_all | solution.py:80
  111.7 4.6 %scatter_custom_fusion = f32[385,512]{1,0:T(8,128)} fusion(s32[512]{0:T(512)S(1)} %bitcast.103, bf16[512,512]{1,0:T(8,128)(2,1)S(1)} %bitcast.79, f32[]{:T(128)} %constant.90.clone.1), kind=kCustom, calls=%fused_computation.33 | custom fusion | flops 524288 | bytes 1312772 | tf_op jit(solution)/shard_map/scatter-add | solution.py:85
  116.3 2.1 fusion.25
  118.4 118.0 %all-reduce.7.cloned.1.call-done = (f32[512,2048]{1,0:T(8,128)}, f32[512,512]{1,0:T(8,128)}) async-done(((f32[512,2048]{1,0:T(8,128)}, f32[512,512]{1,0:T(8,128)}), (f32[512,2048]{1,0:T(8,128)}, f32[512,512]{1,0:T(8,128)})) %all-reduce.7.cloned.1.call-update) | async-done | bytes 5242896 | tf_op jit(solution)/shard_map/psum | solution.py:97
  236.3 4.8 %copy.54 = f32[512,2048]{1,0:T(8,128)} copy(f32[512,2048]{1,0:T(8,128)} %get-tuple-element.33) | data formatting | bytes 8388608
  (89 shorter events, 15.8 us)
Async XLA Ops:
  7.2 44.3 %copy-start = (bf16[512,2048]{1,0:T(8,128)(2,1)S(1)}, bf16[512,2048]{1,0:T(8,128)(2,1)}, u32[]{:S(2)}) copy-start(bf16[512,2048]{1,0:T(8,128)(2,1)} %param.11) | copy-start | bytes 6291460
  7.2 21.5 %copy-start.1 = (bf16[384,512]{1,0:T(8,128)(2,1)S(1)}, bf16[384,512]{1,0:T(8,128)(2,1)}, u32[]{:S(2)}) copy-start(bf16[384,512]{1,0:T(8,128)(2,1)} %param.7) | copy-start | bytes 1179652
  30.7 4.0 %copy-start.17 = (s32[1,256,1]{1,2,0:T(1,128)S(1)}, s32[1,256,1]{1,2,0:T(1,128)}, u32[]{:S(2)}) copy-start(s32[1,256,1]{1,2,0:T(1,128)} %param.8) | copy-start | bytes 3076
  30.7 4.1 %copy-start.18 = (s32[1,256]{1,0:T(1,128)S(1)}, s32[1,256]{1,0:T(1,128)}, u32[]{:S(2)}) copy-start(s32[1,256]{1,0:T(1,128)} %param.10) | copy-start | bytes 3076
  31.7 18.2 %all-to-all-start.1 = ((bf16[32,16,512]{2,1,0:T(8,128)(2,1)}), bf16[32,16,512]{2,1,0:T(8,128)(2,1)S(1)}, u32[]{:S(2)}, u32[]{:S(2)}) async-start(bf16[32,16,512]{2,1,0:T(8,128)(2,1)} %select_select_fusion.1), calls=%async_computation.1 | async-start | bytes 1048576 | tf_op jit(solution)/shard_map/all_to_all | solution.py:68
  34.3 202.0 %all-reduce.7.cloned.1.call-start = ((), (), s32[]{:S(2)}) async-start(), calls=%async_computation.3 | async-start | bytes 10485760 | tf_op jit(solution)/shard_map/psum | solution.py:97
  53.7 1.0 copy-start.4
  54.9 2.4 copy-start.8
  55.0 2.3 copy-start.10
  55.2 2.1 copy-start.5
  57.3 1.0 copy-start.2
  60.1 4.6 %copy-start.6 = (bf16[256,512]{0,1:T(8,128)(2,1)S(1)}, bf16[256,512]{0,1:T(8,128)(2,1)}, u32[]{:S(2)}) copy-start(bf16[256,512]{0,1:T(8,128)(2,1)} %copy-done.5) | copy-start | bytes 786436
  62.4 2.3 copy-start.14
  64.7 3.0 %copy-start.9 = (bf16[256,512]{0,1:T(8,128)(2,1)S(1)}, bf16[256,512]{0,1:T(8,128)(2,1)}, u32[]{:S(2)}) copy-start(bf16[256,512]{0,1:T(8,128)(2,1)} %copy-done.8) | copy-start | bytes 786436
  64.7 4.2 %copy-start.11 = (bf16[256,512]{0,1:T(8,128)(2,1)S(1)}, bf16[256,512]{0,1:T(8,128)(2,1)}, u32[]{:S(2)}) copy-start(bf16[256,512]{0,1:T(8,128)(2,1)} %copy-done.10) | copy-start | bytes 786436
  67.7 2.2 copy-start.12
  67.7 5.7 %copy-start.3 = (bf16[1,256,512]{2,1,0:T(8,128)(2,1)S(1)}, bf16[1,256,512]{2,1,0:T(8,128)(2,1)}, u32[]{:S(2)}) copy-start(bf16[1,256,512]{2,1,0:T(8,128)(2,1)} %param.13) | copy-start | bytes 786436
  68.9 3.7 %copy-start.13 = (bf16[8,256,64]{1,2,0:T(8,128)(2,1)S(1)}, bf16[8,256,64]{1,2,0:T(8,128)(2,1)}, u32[]{:S(2)}) copy-start(bf16[8,256,64]{1,2,0:T(8,128)(2,1)} %fusion.44) | copy-start | bytes 786436
  70.7 4.0 %copy-start.15 = (bf16[256,512]{1,0:T(8,128)(2,1)S(1)}, bf16[256,512]{1,0:T(8,128)(2,1)}, u32[]{:S(2)}) copy-start(bf16[256,512]{1,0:T(8,128)(2,1)} %get-tuple-element.11) | copy-start | bytes 786436
  79.8 0.9 copy-start.16
  87.6 24.1 %all-to-all-start.2 = ((bf16[32,16,512]{2,1,0:T(8,128)(2,1)}), bf16[32,16,512]{2,1,0:T(8,128)(2,1)S(1)}, u32[]{:S(2)}, u32[]{:S(2)}) async-start(bf16[32,16,512]{2,1,0:T(8,128)(2,1)} %select_select_fusion), calls=%async_computation.2 | async-start | bytes 1048576 | tf_op jit(solution)/shard_map/all_to_all | solution.py:80
  236.3 4.8 %copy-start.7 = (f32[512,512]{1,0:T(8,128)S(1)}, f32[512,512]{1,0:T(8,128)}, u32[]{:S(2)}) copy-start(f32[512,512]{1,0:T(8,128)} %get-tuple-element.34) | copy-start | bytes 3145732
Sparse Core Ops, SparseCore 0:
  79.9 156.3 all-reduce.6

commit v2 on v1

--- a/solution.py
+++ b/solution.py
@@ -1,6 +1,10 @@
+import functools
+
 import jax
 import jax.numpy as jnp
 from jax import lax
+from jax.experimental import pallas as pl
+from jax.experimental.pallas import tpu as pltpu
 from jax.sharding import PartitionSpec as P
 
 HEADS = 8
@@ -41,6 +45,144 @@
         gated, w_out, preferred_element_type=jnp.float32
     )
     return result.astype(jnp.bfloat16)
+
+
+def share_parts(wide, narrow):
+    third = (wide + narrow) // 3 // 128 * 128 + 128
+    rest = wide - 2 * third
+    return (
+        (0, 0, third, 0, 0),
+        (0, third, third, third, 1),
+        (0, 2 * third, rest, 2 * third, 2),
+        (1, 0, narrow, wide, 2),
+    )
+
+
+def sum_shares_kernel(
+    shards, parts, in_ref, out_ref, sum_in_ref, sum_out_ref,
+    work, landing, gathered, send_sem, recv_sem, back_send_sem, back_recv_sem,
+):
+    rows, wide = in_ref.shape
+    me = lax.axis_index("table")
+    levels = shards.bit_length() - 1
+    sources = (in_ref, out_ref)
+
+    def side(bit):
+        return (me // (1 << bit)) % 2
+
+    def partner(bit):
+        return me + (1 - 2 * side(bit)) * (1 << bit)
+
+    barrier = pltpu.get_barrier_semaphore()
+    for bit in range(levels):
+        pl.semaphore_signal(
+            barrier, inc=1, device_id={"table": partner(bit)}, device_id_type=pl.DeviceIdType.MESH
+        )
+    pl.semaphore_wait(barrier, levels)
+
+    orders = []
+    for part in parts:
+        far = list(range(1, levels))
+        orders.append([0] + far[part[4]:] + far[: part[4]])
+
+    def rows_at(start, count):
+        return pl.ds(pl.multiple_of(start, 16), count)
+
+    bases = [[0] for _ in parts]
+
+    def start_sum(p, step):
+        source, first, columns, place, _ = parts[p]
+        bit, half = orders[p][step], rows >> (step + 1)
+        base = bases[p][step]
+        bases[p].append(base + side(bit) * half)
+        going = rows_at(base + (1 - side(bit)) * half, half)
+        if step == 0:
+            block = sources[source].at[going, pl.ds(first, columns)]
+        else:
+            block = work.at[going, pl.ds(place, columns)]
+        copy = pltpu.make_async_remote_copy(
+            src_ref=block,
+            dst_ref=landing.at[pl.ds(rows - 2 * half, half), pl.ds(place, columns)],
+            send_sem=send_sem.at[p, step],
+            recv_sem=recv_sem.at[p, step],
+            device_id={"table": partner(bit)},
+            device_id_type=pl.DeviceIdType.MESH,
+        )
+        copy.start()
+        return copy
+
+    def start_back(p, step):
+        _, _, columns, place, _ = parts[p]
+        half = rows >> (step + 1)
+        block = gathered.at[rows_at(bases[p][step + 1], half), pl.ds(place, columns)]
+        copy = pltpu.make_async_remote_copy(
+            src_ref=block,
+            dst_ref=block,
+            send_sem=back_send_sem.at[p, step],
+            recv_sem=back_recv_sem.at[p, step],
+            device_id={"table": partner(orders[p][step])},
+            device_id_type=pl.DeviceIdType.MESH,
+        )
+        copy.start()
+        return copy
+
+    flying = [start_sum(p, 0) for p in range(len(parts))]
+    for step in range(levels):
+        half = rows >> (step + 1)
+        for p, (source, first, columns, place, _) in enumerate(parts):
+            flying[p].wait()
+            kept = rows_at(bases[p][step + 1], half)
+            here = slice(place, place + columns)
+            if step == 0:
+                own = sources[source][kept, first : first + columns]
+            else:
+                own = work[kept, here]
+            other = landing[rows - 2 * half : rows - half, here]
+            total = (own.astype(jnp.float32) + other.astype(jnp.float32)).astype(jnp.bfloat16)
+            if step + 1 < levels:
+                work[kept, here] = total
+                flying[p] = start_sum(p, step + 1)
+            else:
+                gathered[kept, here] = total
+                flying[p] = start_back(p, step)
+    for step in reversed(range(levels)):
+        for p in range(len(parts)):
+            flying[p].wait()
+            if step > 0:
+                flying[p] = start_back(p, step - 1)
+    sum_in_ref[...] = gathered[:, :wide]
+    sum_out_ref[...] = gathered[:, wide:]
+
+
+def sum_shares(shards, d_in, d_out):
+    rows, wide = d_in.shape
+    narrow = d_out.shape[1]
+    parts = share_parts(wide, narrow)
+    levels = shards.bit_length() - 1
+    joined = (rows, wide + narrow)
+    vmem = pl.BlockSpec(memory_space=pltpu.VMEM)
+    sums = pl.pallas_call(
+        functools.partial(sum_shares_kernel, shards, parts),
+        out_shape=(
+            jax.ShapeDtypeStruct(d_in.shape, jnp.bfloat16),
+            jax.ShapeDtypeStruct(d_out.shape, jnp.bfloat16),
+        ),
+        in_specs=[vmem, vmem],
+        out_specs=(vmem, vmem),
+        scratch_shapes=[
+            pltpu.VMEM(joined, jnp.bfloat16),
+            pltpu.VMEM(joined, jnp.bfloat16),
+            pltpu.VMEM(joined, jnp.bfloat16),
+        ]
+        + [pltpu.SemaphoreType.DMA((len(parts), levels))] * 4,
+        compiler_params=pltpu.CompilerParams(
+            collective_id=0, has_side_effects=True, vmem_limit_bytes=32 * 2**20
+        ),
+        cost_estimate=pl.CostEstimate(
+            flops=rows * (wide + narrow), bytes_accessed=100 * 2**20, transcendentals=0
+        ),
+    )(d_in, d_out)
+    return sums[0].astype(jnp.float32), sums[1].astype(jnp.float32)
 
 
 def on_device(table, owner, row_in_shard, segment, w_in, w_out, cotangent):
@@ -86,15 +228,20 @@
         flat_grads.astype(jnp.float32), table_ids, num_segments=vocab_rows + 1
     )[:vocab_rows]
     grad_table = lax.psum(partial_sum.astype(jnp.bfloat16), "dp").astype(jnp.float32)
-    share_in, share_out = (
-        lax.psum_scatter(
-            d_in.astype(jnp.float32).astype(jnp.bfloat16), "dp", scatter_dimension=1, tiled=True
-        ).astype(jnp.float32),
-        lax.psum_scatter(
-            d_out.astype(jnp.float32).astype(jnp.bfloat16), "dp", scatter_dimension=0, tiled=True
-        ).astype(jnp.float32),
-    )
-    grad_w_in, grad_w_out = lax.psum((share_in, share_out), "table")
+    copies = lax.axis_size("dp")
+    rows = d_in.shape[0]
+    if copies == 1 and shards & (shards - 1) == 0 and rows % (16 * shards) == 0:
+        grad_w_in, grad_w_out = sum_shares(shards, d_in, d_out)
+    else:
+        share_in, share_out = (
+            lax.psum_scatter(
+                d_in.astype(jnp.float32).astype(jnp.bfloat16), "dp", scatter_dimension=1, tiled=True
+            ).astype(jnp.float32),
+            lax.psum_scatter(
+                d_out.astype(jnp.float32).astype(jnp.bfloat16), "dp", scatter_dimension=0, tiled=True
+            ).astype(jnp.float32),
+        )
+        grad_w_in, grad_w_out = lax.psum((share_in, share_out), "table")
     return (layer_rows[None], grad_table, grad_w_in, grad_w_out)
 
 

time: 250 us -> 136 us (0.54)
  waiting for transfers between devices: 152 us -> 15 us
  Pallas kernels: 0 us -> 48.1 us
  between operations: 14.4 us -> 1.12 us
  local copies, waits for them, and re-layouts: 22.1 us -> 13.2 us
  matrix products: 25.5 us -> 19.4 us
  other arithmetic: 14.8 us -> 18.4 us
    psum x1 -> x0, waiting for transfers between devices: 118 us -> none  [on_device(): grad_w_in, grad_w_out = lax.psum((share_in, share_out), 'table')]
    pallas_call x0 -> x1, Pallas kernels: none -> 48.1 us  [sum_shares(): pl.pallas_call(functools.partial(sum_shares_kernel, shards, parts), out_s...]
    all_to_all x1, waiting for transfers between devices: 18.9 us -> 0.01 us  [on_device(): lax.all_to_all(sent_grads.reshape(shards, capacity, -1), 'table', split_a...]
    unnamed x40 -> x36, local copies, waits for them, and re-layouts: 8.13 us -> 1.57 us
    convert_element_type x0 -> x2, other arithmetic: none -> 3.64 us  [sum_shares(): return (sums[0].astype(jnp.float32), sums[1].astype(jnp.float32))]
  transfers between devices with their start and end apart: 3 -> 2, of which waited for: 3 -> 1; matrix products, arithmetic and copies ran while one was open for 6% -> 6% of each run, Pallas kernels for 0% -> 36%
where the time goes in v2:
time: 136 us; the launch traced here: 135 us
  Pallas kernels  48.1 us (35%)
  matrix products  19.4 us (14%)
  other arithmetic  18.4 us (14%)
  waiting for transfers between devices  15 us (11%)
  blocking collectives  14.3 us (11%)
  local copies, waits for them, and re-layouts  13.2 us (10%)
  starting transfers between devices  5.98 us (4%)
    pallas_call x1, Pallas kernels, sum_shares(): pl.pallas_call(functools.partial(sum_shares_kernel, shards, parts), out_s...  48.1 us
    all_to_all x1, waiting for transfers between devices, on_device(): lax.all_to_all(found_rows, 'table', split_axis=0, concat_axis=0, tiled=True)  15 us
    all_to_all x1, blocking collectives, on_device(): lax.all_to_all(request, 'table', split_axis=0, concat_axis=0, tiled=True)  14.3 us
    dot_general x3, matrix products, hstu_layer(): jnp.dot(normed, w_in, preferred_element_type=jnp.float32)  8.68 us
    dot_general x3, matrix products, hstu_layer(): jnp.einsum('hqk,khd->qhd', weights, value_part, preferred_element_type=jn...  4.86 us
    scatter-add x1, other arithmetic, on_device(): jax.ops.segment_sum(flat_grads.astype(jnp.float32), table_ids, num_segmen...  4.56 us
    gather x2, local copies, waits for them, and re-layouts, on_device(): jnp.take(local_row, source_row)  3.7 us
    convert_element_type x2, other arithmetic, sum_shares(): return (sums[0].astype(jnp.float32), sums[1].astype(jnp.float32))  3.64 us
  transfers between devices with their start and end apart: 2, of which 1 were waited for; matrix products, arithmetic and copies ran while one was open for 6% of the time, Pallas kernels for 36%

profile of v2, /device:TPU:0, one launch (start us, length us, event | category | flops | bytes accessed | tf_op | source)
XLA Modules:
  0.0 135.5 jit_solution(9407009302130061560)
XLA Ops:
  0.7 1.0 convert_reduce_fusion.1
  2.9 3.6 %gather_fusion = s32[512]{0:T(512)S(1)} fusion(s32[256]{0:T(256)} %bitcast.76, s32[1024]{0:T(1024)S(1)} %pad_clamp_fusion.2), kind=kCustom, calls=%fused_computation | custom fusion | bytes 6144 | tf_op jit(solution)/shard_map/jit(_take)/gather | solution.py:203
  6.6 14.3 %all_to_all.19 = s32[32,1,16]{2,1,0:T(1,128)S(1)} all-to-all(s32[32,1,16]{2,1,0:T(1,128)S(1)} %bitcast.94), channel_id=1, replica_groups=mesh['table'=32,'dp'=1] {'table'}, dimensions={0} | all-to-all | bytes 4096 | tf_op jit(solution)/shard_map/all_to_all | solution.py:204
  22.2 2.0 %gather_fusion.1 = bf16[512,512]{1,0:T(8,128)(2,1)S(1)} fusion(bf16[384,512]{1,0:T(8,128)(2,1)S(1)} %copy-done.1, s32[1024]{0:T(1024)S(1)} %pad_clamp_fusion.1), kind=kCustom, calls=%fused_computation.1 | custom fusion | bytes 1050624 | tf_op jit(solution)/shard_map/jit(_take)/gather | solution.py:206
  24.2 1.0 select_select_fusion.1
  25.2 2.8 %all-to-all-start.1 = ((bf16[32,16,512]{2,1,0:T(8,128)(2,1)}), bf16[32,16,512]{2,1,0:T(8,128)(2,1)S(1)}, u32[]{:S(2)}, u32[]{:S(2)}) async-start(bf16[32,16,512]{2,1,0:T(8,128)(2,1)} %select_select_fusion.1), calls=%async_computation.1 | async-start | bytes 1048576 | tf_op jit(solution)/shard_map/all_to_all | solution.py:210
  28.3 15.0 %all-to-all-done.1 = bf16[32,16,512]{2,1,0:T(8,128)(2,1)S(1)} async-done(((bf16[32,16,512]{2,1,0:T(8,128)(2,1)}), bf16[32,16,512]{2,1,0:T(8,128)(2,1)S(1)}, u32[]{:S(2)}, u32[]{:S(2)}) %all-to-all-start.1) | async-done | bytes 524320 | tf_op jit(solution)/shard_map/all_to_all | solution.py:210
  43.4 1.2 gather_fusion.2
  45.0 2.1 %multiply_convert_fusion = (bf16[256,2048]{1,0:T(8,128)(2,1)S(1)}, f32[256,2048]{1,0:T(8,128)}) fusion(bf16[512,2048]{1,0:T(8,128)(2,1)S(1)} %copy-done, f32[256]{0:T(256)S(1)} %fusion.30, f32[256]{0:T(256)S(1)} %broadcast_multiply_fusion.1, bf16[256,512]{1,0:T(8,128)(2,1)S(1)} %gather_fusion.2, pred[256]{0:T(512)(128)(4,1)S(1)} %get-tuple-element.10), kind=kOutput, calls=%fused_computation.17 | convolution fusion | flops 540147712 | bytes 5507328 | tf_op jit(solution)/shard_map/jvp()/dot_general | solution.py:27
  48.6 2.1 %select_convert_fusion = (bf16[8,256,256]{2,1,0:T(8,128)(2,1)S(1)}, f32[8,256,256]{2,1,0:T(8,128)}) fusion(pred[256,256]{1,0:T(8,128)(4,1)S(1)} %fusion.28, bf16[256,8,64]{0,2,1:T(8,128)(2,1)S(1)} %bitcast.84, bf16[256,8,64]{0,2,1:T(8,128)(2,1)S(1)} %bitcast.86), kind=kOutput, calls=%fused_computation.15 | convolution fusion | flops 70778880 | bytes 3735552 | tf_op jit(solution)/shard_map/jvp(qhd,khd->hqk)/dot_general | solution.py:36
  52.1 1.6 %multiply_reduce_fusion = (f32[256]{0:T(256)S(1)}, f32[256,512]{1,0:T(8,128)S(1)}) fusion(f32[256,512]{1,0:T(8,128)S(1)} %copy.47, f32[256]{0:T(256)S(1)} %broadcast_multiply_fusion, bf16[256,2048]{1,0:T(8,128)(2,1)} %copy-done.4, bf16[512,512]{1,0:T(8,128)(2,1)} %param.12, bf16[1,256,512]{2,1,0:T(8,128)(2,1)} %param.13), kind=kOutput, calls=%fused_computation.54 | convolution fusion | flops 135134976 | bytes 2099200 | tf_op jit(solution)/shard_map/transpose(jvp())/dot_general | solution.py:44
  53.7 2.0 %fusion.38 = (f32[256]{0:T(256)S(1)}, f32[256,512]{1,0:T(8,128)S(1)}, bf16[256,512]{1,0:T(8,128)(2,1)}, bf16[256,512]{1,0:T(8,128)(2,1)S(1)}) fusion(f32[256]{0:T(256)S(1)} %get-tuple-element.21, f32[256,512]{1,0:T(8,128)S(1)} %copy.47, f32[256]{0:T(256)S(1)} %broadcast_multiply_fusion, f32[256]{0:T(256)S(1)} %get-tuple-element.22, ...), kind=kLoop, calls=%fused_computation.101 | loop fusion | flops 1703680 | bytes 2363392 | tf_op jit(solution)/shard_map/transpose(jvp())/reduce_sum | solution.py:18
  56.0 1.5 %fusion.41 = bf16[8,64,256]{2,1,0:T(8,128)(2,1)S(1)} fusion(bf16[8,64,256]{2,1,0:T(8,128)(2,1)S(1)} %bitcast.89, bf16[8,256,256]{2,1,0:T(8,128)(2,1)} %copy-done.2), kind=kOutput, calls=%fused_computation.104 | convolution fusion | flops 67108864 | bytes 1572864 | tf_op jit(solution)/shard_map/transpose(jvp(hqk,khd->qhd))/dot_general | solution.py:40
  57.5 2.9 %fusion.4 = bf16[8,256,256]{2,1,0:T(8,128)(2,1)S(1)} fusion(f32[8,256,256]{2,1,0:T(8,128)} %get-tuple-element.26, bf16[8,64,256]{2,1,0:T(8,128)(2,1)S(1)} %bitcast.90, bf16[256,8,64]{0,2,1:T(8,128)(2,1)S(1)} %bitcast.83, pred[256,256]{1,0:T(8,128)(4,1)S(1)} %fusion.28), kind=kOutput, calls=%fused_computation.14 | convolution fusion | flops 74448896 | bytes 3735552 | tf_op jit(solution)/shard_map/transpose(jvp(hqk,khd->qhd))/dot_general | solution.py:40
  62.4 3.3 %fusion.18 = (f32[256]{0:T(256)S(1)}, f32[256,512]{1,0:T(8,128)S(1)}) fusion(f32[256]{0:T(256)S(1)} %broadcast_multiply_fusion.1, bf16[256,512]{1,0:T(8,128)(2,1)S(1)} %gather_fusion.2, pred[256]{0:T(512)(128)(4,1)S(1)} %get-tuple-element.10, bf16[512,2048]{1,0:T(8,128)(2,1)S(1)} %copy-done, f32[256,2048]{1,0:T(8,128)} %get-tuple-element.24, ...), kind=kOutput, calls=%fused_computation.47 | convolution fusion | flops 546701056 | bytes 6031616 | tf_op jit(solution)/shard_map/transpose(jvp())/dot_general | solution.py:27
  66.3 2.0 %gather_fusion.3 = bf16[512,512]{1,0:T(8,128)(2,1)S(1)} fusion(bf16[256,512]{1,0:T(8,128)(2,1)S(1)} %fusion.24, s32[1024]{0:T(1024)S(1)} %pad_clamp_fusion.2), kind=kCustom, calls=%fused_computation.3 | custom fusion | bytes 1050624 | tf_op jit(solution)/shard_map/jit(_take)/gather | solution.py:220
  69.3 3.2 %all-to-all-start.2 = ((bf16[32,16,512]{2,1,0:T(8,128)(2,1)}), bf16[32,16,512]{2,1,0:T(8,128)(2,1)S(1)}, u32[]{:S(2)}, u32[]{:S(2)}) async-start(bf16[32,16,512]{2,1,0:T(8,128)(2,1)} %select_select_fusion), calls=%async_computation.2 | async-start | bytes 1048576 | tf_op jit(solution)/shard_map/all_to_all | solution.py:222
  72.9 3.2 %convolution_convert_fusion.in_ref = bf16[512,2048]{1,0:T(8,128)(2,1)S(1)} fusion(f32[256]{0:T(256)S(1)} %fusion.30, f32[256]{0:T(256)S(1)} %broadcast_multiply_fusion.1, bf16[256,512]{1,0:T(8,128)(2,1)S(1)} %gather_fusion.2, pred[256]{0:T(512)(128)(4,1)S(1)} %get-tuple-element.10, f32[256,2048]{1,0:T(8,128)} %get-tuple-element.24, ...), kind=kOutput, calls=%fused_computation.7 | convolution fusion | flops 547487744 | bytes 5507328 | tf_op jit(solution)/shard_map/transpose(jvp())/dot_general | solution.py:27
  76.1 48.1 %shard_map.102 = (bf16[512,2048]{1,0:T(8,128)(2,1)S(1)}, bf16[512,512]{1,0:T(8,128)(2,1)S(1)}) custom-call(bf16[512,2048]{1,0:T(8,128)(2,1)S(1)} %convolution_convert_fusion.in_ref, bf16[512,512]{1,0:T(8,128)(2,1)S(1)} %convolution_convert_fusion.2.out_ref), custom_call_target="tpu_custom_call" | custom-call | flops 1310720 | bytes 104857600 | tf_op jit(solution)/shard_map/pallas_call | solution.py:164
  124.2 2.5 %convert_element_type.122 = f32[512,2048]{1,0:T(8,128)} convert(bf16[512,2048]{1,0:T(8,128)(2,1)S(1)} %get-tuple-element.6) | non-fusion elementwise | flops 1048576 | bytes 6291456 | tf_op jit(solution)/shard_map/convert_element_type | solution.py:185
  126.7 1.1 convert_element_type.123
  127.8 1.0 fusion.8
  128.9 4.6 %scatter_custom_fusion = f32[385,512]{1,0:T(8,128)} fusion(s32[512]{0:T(512)S(1)} %bitcast.103, bf16[512,512]{1,0:T(8,128)(2,1)S(1)} %bitcast.79, f32[]{:T(128)} %constant.90.clone.1), kind=kCustom, calls=%fused_computation.31 | custom fusion | flops 524288 | bytes 1312772 | tf_op jit(solution)/shard_map/scatter-add | solution.py:227
  133.4 2.1 %fusion.23 = f32[384,512]{1,0:T(8,128)} fusion(f32[385,512]{1,0:T(8,128)} %scatter_custom_fusion), kind=kLoop, calls=%fused_computation.60 | loop fusion | flops 196608 | bytes 1179648 | tf_op jit(solution)/shard_map/convert_element_type | solution.py:230
  (85 shorter events, 10.1 us)
Async XLA Ops:
  0.6 44.4 %copy-start = (bf16[512,2048]{1,0:T(8,128)(2,1)S(1)}, bf16[512,2048]{1,0:T(8,128)(2,1)}, u32[]{:S(2)}) copy-start(bf16[512,2048]{1,0:T(8,128)(2,1)} %param.11) | copy-start | bytes 6291460
  0.6 21.5 %copy-start.1 = (bf16[384,512]{1,0:T(8,128)(2,1)S(1)}, bf16[384,512]{1,0:T(8,128)(2,1)}, u32[]{:S(2)}) copy-start(bf16[384,512]{1,0:T(8,128)(2,1)} %param.7) | copy-start | bytes 1179652
  24.2 4.0 %copy-start.16 = (s32[1,256,1]{1,2,0:T(1,128)S(1)}, s32[1,256,1]{1,2,0:T(1,128)}, u32[]{:S(2)}) copy-start(s32[1,256,1]{1,2,0:T(1,128)} %param.8) | copy-start | bytes 3076
  24.2 4.0 %copy-start.17 = (s32[1,256]{1,0:T(1,128)S(1)}, s32[1,256]{1,0:T(1,128)}, u32[]{:S(2)}) copy-start(s32[1,256]{1,0:T(1,128)} %param.10) | copy-start | bytes 3076
  25.2 18.2 %all-to-all-start.1 = ((bf16[32,16,512]{2,1,0:T(8,128)(2,1)}), bf16[32,16,512]{2,1,0:T(8,128)(2,1)S(1)}, u32[]{:S(2)}, u32[]{:S(2)}) async-start(bf16[32,16,512]{2,1,0:T(8,128)(2,1)} %select_select_fusion.1), calls=%async_computation.1 | async-start | bytes 1048576 | tf_op jit(solution)/shard_map/all_to_all | solution.py:210
  47.1 1.0 copy-start.4
  48.3 2.5 %copy-start.5 = (bf16[256,512]{0,1:T(8,128)(2,1)}, bf16[256,512]{0,1:T(8,128)(2,1)S(1)}, u32[]{:S(2)}) copy-start(bf16[256,512]{0,1:T(8,128)(2,1)S(1)} %copy.44) | copy-start | bytes 786436
  48.5 2.3 %copy-start.8 = (bf16[256,512]{0,1:T(8,128)(2,1)}, bf16[256,512]{0,1:T(8,128)(2,1)S(1)}, u32[]{:S(2)}) copy-start(bf16[256,512]{0,1:T(8,128)(2,1)S(1)} %copy.45) | copy-start | bytes 786436
  48.6 2.2 %copy-start.10 = (bf16[256,512]{0,1:T(8,128)(2,1)}, bf16[256,512]{0,1:T(8,128)(2,1)S(1)}, u32[]{:S(2)}) copy-start(bf16[256,512]{0,1:T(8,128)(2,1)S(1)} %copy.46) | copy-start | bytes 786436
  50.8 1.0 copy-start.2
  53.7 3.8 %copy-start.6 = (bf16[256,512]{0,1:T(8,128)(2,1)S(1)}, bf16[256,512]{0,1:T(8,128)(2,1)}, u32[]{:S(2)}) copy-start(bf16[256,512]{0,1:T(8,128)(2,1)} %copy-done.5) | copy-start | bytes 786436
  55.7 6.6 %copy-start.13 = (bf16[256,512]{1,0:T(8,128)(2,1)}, bf16[256,512]{1,0:T(8,128)(2,1)S(1)}, u32[]{:S(2)}) copy-start(bf16[256,512]{1,0:T(8,128)(2,1)S(1)} %get-tuple-element.13) | copy-start | bytes 786436
  57.5 2.9 %copy-start.11 = (bf16[256,512]{0,1:T(8,128)(2,1)S(1)}, bf16[256,512]{0,1:T(8,128)(2,1)}, u32[]{:S(2)}) copy-start(bf16[256,512]{0,1:T(8,128)(2,1)} %copy-done.10) | copy-start | bytes 786436
  57.5 3.3 %copy-start.9 = (bf16[256,512]{0,1:T(8,128)(2,1)S(1)}, bf16[256,512]{0,1:T(8,128)(2,1)}, u32[]{:S(2)}) copy-start(bf16[256,512]{0,1:T(8,128)(2,1)} %copy-done.8) | copy-start | bytes 786436
  62.2 3.5 %copy-start.14 = (bf16[256,512]{1,0:T(8,128)(2,1)}, bf16[256,512]{1,0:T(8,128)(2,1)S(1)}, u32[]{:S(2)}) copy-start(bf16[256,512]{1,0:T(8,128)(2,1)S(1)} %copy.50) | copy-start | bytes 786436
  62.3 3.4 %copy-start.15 = (bf16[256,512]{1,0:T(8,128)(2,1)}, bf16[256,512]{1,0:T(8,128)(2,1)S(1)}, u32[]{:S(2)}) copy-start(bf16[256,512]{1,0:T(8,128)(2,1)S(1)} %copy.49) | copy-start | bytes 786436
  62.3 3.7 %copy-start.3 = (bf16[1,256,512]{2,1,0:T(8,128)(2,1)S(1)}, bf16[1,256,512]{2,1,0:T(8,128)(2,1)}, u32[]{:S(2)}) copy-start(bf16[1,256,512]{2,1,0:T(8,128)(2,1)} %param.13) | copy-start | bytes 786436
  68.3 4.2 %copy-start.7 = (bf16[256,512]{1,0:T(8,128)(2,1)S(1)}, bf16[256,512]{1,0:T(8,128)(2,1)}, u32[]{:S(2)}) copy-start(bf16[256,512]{1,0:T(8,128)(2,1)} %get-tuple-element.12) | copy-start | bytes 786436
  69.3 59.5 %all-to-all-start.2 = ((bf16[32,16,512]{2,1,0:T(8,128)(2,1)}), bf16[32,16,512]{2,1,0:T(8,128)(2,1)S(1)}, u32[]{:S(2)}, u32[]{:S(2)}) async-start(bf16[32,16,512]{2,1,0:T(8,128)(2,1)} %select_select_fusion), calls=%async_computation.2 | async-start | bytes 1048576 | tf_op jit(solution)/shard_map/all_to_all | solution.py:222
  124.2 3.7 %copy-start.12 = (bf16[512,512]{1,0:T(8,128)(2,1)S(1)}, bf16[512,512]{1,0:T(8,128)(2,1)}, u32[]{:S(2)}) copy-start(bf16[512,512]{1,0:T(8,128)(2,1)} %param.12) | copy-start | bytes 1572868

commit v3 on v2

--- a/solution.py
+++ b/solution.py
@@ -198,15 +198,14 @@
     rank_own = jnp.sum(earlier.astype(jnp.int32), axis=1)
     slot_index = target * capacity + rank_own
     slot_match = slot_index[None, :] == jnp.arange(slot_total)[:, None]
-    filled = jnp.any(slot_match, axis=1)
     source_row = jnp.sum(jnp.where(slot_match, jnp.arange(row_count)[None, :], 0), axis=1)
-    request = jnp.where(filled, jnp.take(local_row, source_row), -1).reshape(shards, capacity)
+    request = jnp.sum(jnp.where(slot_match, local_row[None, :] + 1, 0), axis=1) - 1
+    request = request.reshape(shards, capacity)
     asked_rows = lax.all_to_all(request, "table", split_axis=0, concat_axis=0, tiled=True)
     is_valid = asked_rows >= 0
     found_rows = jnp.take(table, jnp.maximum(asked_rows, 0).reshape(-1), axis=0).reshape(
         shards, capacity, -1
     )
-    found_rows = jnp.where(is_valid[..., None], found_rows, jnp.zeros((), table.dtype))
     returned = lax.all_to_all(found_rows, "table", split_axis=0, concat_axis=0, tiled=True)
     embedded = jnp.take(returned.reshape(slot_total, -1), slot_index, axis=0)
     seg_rows = segment[0]
@@ -216,17 +215,14 @@
 
     layer_rows, pullback = jax.vjp(local_layer, embedded, w_in, w_out)
     d_emb, d_in, d_out = pullback(cotangent[0])
-    sent_grads = jnp.where(
-        filled[:, None], jnp.take(d_emb, source_row, axis=0), jnp.zeros((), d_emb.dtype)
-    )
+    sent_grads = jnp.take(d_emb, source_row, axis=0)
     arrived = lax.all_to_all(
         sent_grads.reshape(shards, capacity, -1), "table", split_axis=0, concat_axis=0, tiled=True
     )
     flat_grads = arrived.reshape(slot_total, -1)
     table_ids = jnp.where(is_valid, asked_rows, vocab_rows).reshape(-1)
-    partial_sum = jax.ops.segment_sum(
-        flat_grads.astype(jnp.float32), table_ids, num_segments=vocab_rows + 1
-    )[:vocab_rows]
+    row_match = (table_ids[None, :] == jnp.arange(vocab_rows)[:, None]).astype(flat_grads.dtype)
+    partial_sum = jnp.dot(row_match, flat_grads, preferred_element_type=jnp.float32)
     grad_table = lax.psum(partial_sum.astype(jnp.bfloat16), "dp").astype(jnp.float32)
     copies = lax.axis_size("dp")
     rows = d_in.shape[0]

time: 136 us -> 129 us (0.949)
  blocking collectives: 14.3 us -> 0 us
  starting transfers between devices: 5.98 us -> 13.1 us
  waiting for transfers between devices: 15 us -> 21.1 us
  other arithmetic: 18.4 us -> 12.3 us
    all_to_all x1 -> x0, blocking collectives: 14.3 us -> none  [on_device(): lax.all_to_all(request, 'table', split_axis=0, concat_axis=0, tiled=True)]
    all_to_all x0 -> x1, starting transfers between devices: none -> 7.3 us  [on_device(): lax.all_to_all(request, 'table', split_axis=0, concat_axis=0, tiled=True)]
    all_to_all x0 -> x1, waiting for transfers between devices: none -> 7.06 us  [on_device(): lax.all_to_all(request, 'table', split_axis=0, concat_axis=0, tiled=True)]
    scatter-add x1 -> x0, other arithmetic: 4.56 us -> none  [on_device(): jax.ops.segment_sum(flat_grads.astype(jnp.float32), table_ids, num_segmen...]
    gather x3 -> x1, local copies, waits for them, and re-layouts: 5.67 us -> 1.97 us  [on_device(): sent_grads = jnp.take(d_emb, source_row, axis=0)]
    convert_element_type x1 -> x0, other arithmetic: 2.06 us -> none  [on_device(): lax.psum(partial_sum.astype(jnp.bfloat16), 'dp').astype(jnp.float32)]
  transfers between devices with their start and end apart: 2 -> 3, of which waited for: 1 -> 2; matrix products, arithmetic and copies ran while one was open for 6% -> 7% of each run, Pallas kernels for 36% -> 38%
where the time goes in v3:
time: 129 us; the launch traced here: 128 us
  Pallas kernels  48.1 us (37%)
  waiting for transfers between devices  21.1 us (16%)
  matrix products  20.7 us (16%)
  starting transfers between devices  13.1 us (10%)
  other arithmetic  12.3 us (10%)
  local copies, waits for them, and re-layouts  11.9 us (9%)
    pallas_call x1, Pallas kernels, sum_shares(): pl.pallas_call(functools.partial(sum_shares_kernel, shards, parts), out_s...  48.1 us
    all_to_all x1, waiting for transfers between devices, on_device(): lax.all_to_all(found_rows, 'table', split_axis=0, concat_axis=0, tiled=True)  14 us
    dot_general x3, matrix products, hstu_layer(): jnp.dot(normed, w_in, preferred_element_type=jnp.float32)  8.72 us
    all_to_all x1, starting transfers between devices, on_device(): lax.all_to_all(request, 'table', split_axis=0, concat_axis=0, tiled=True)  7.3 us
    all_to_all x1, waiting for transfers between devices, on_device(): lax.all_to_all(request, 'table', split_axis=0, concat_axis=0, tiled=True)  7.06 us
    dot_general x3, matrix products, hstu_layer(): jnp.einsum('hqk,khd->qhd', weights, value_part, preferred_element_type=jn...  4.86 us
    convert_element_type x2, other arithmetic, sum_shares(): return (sums[0].astype(jnp.float32), sums[1].astype(jnp.float32))  3.64 us
    all_to_all x1, starting transfers between devices, on_device(): lax.all_to_all(sent_grads.reshape(shards, capacity, -1), 'table', split_a...  3.15 us
  transfers between devices with their start and end apart: 3, of which 2 were waited for; matrix products, arithmetic and copies ran while one was open for 7% of the time, Pallas kernels for 38%

profile of v3, /device:TPU:0, one launch (start us, length us, event | category | flops | bytes accessed | tf_op | source)
XLA Modules:
  0.0 128.1 jit_solution(4702828390238127787)
XLA Ops:
  0.6 1.0 convert_reduce_fusion.1
  4.0 7.3 %all-to-all-start = ((s32[32,1,16]{2,1,0:T(1,128)}), s32[32,1,16]{2,1,0:T(1,128)S(1)}, u32[]{:S(2)}, u32[]{:S(2)}) async-start(s32[32,1,16]{2,1,0:T(1,128)} %bitcast.2), calls=%async_computation | async-start | bytes 32768 | tf_op jit(solution)/shard_map/all_to_all | solution.py:204
  11.3 7.1 %all-to-all-done = s32[32,1,16]{2,1,0:T(1,128)S(1)} async-done(((s32[32,1,16]{2,1,0:T(1,128)}), s32[32,1,16]{2,1,0:T(1,128)S(1)}, u32[]{:S(2)}, u32[]{:S(2)}) %all-to-all-start) | async-done | bytes 2080 | tf_op jit(solution)/shard_map/all_to_all | solution.py:204
  18.7 3.0 %gather_fusion = bf16[512,512]{1,0:T(8,128)(2,1)S(1)} fusion(bf16[384,512]{1,0:T(8,128)(2,1)} %param.7, s32[1024]{0:T(1024)S(1)} %pad_clamp_fusion.2), kind=kCustom, calls=%fused_computation | custom fusion | bytes 1050624 | tf_op jit(solution)/shard_map/jit(_take)/gather | solution.py:206
  21.8 0.9 broadcast_select_fusion.1
  22.7 2.6 %all-to-all-start.1 = ((bf16[32,16,512]{2,1,0:T(8,128)(2,1)}), bf16[32,16,512]{2,1,0:T(8,128)(2,1)S(1)}, u32[]{:S(2)}, u32[]{:S(2)}) async-start(bf16[32,16,512]{2,1,0:T(8,128)(2,1)} %broadcast_select_fusion.1), calls=%async_computation.1 | async-start | bytes 1048576 | tf_op jit(solution)/shard_map/all_to_all | solution.py:209
  26.9 14.0 %all-to-all-done.1 = bf16[32,16,512]{2,1,0:T(8,128)(2,1)S(1)} async-done(((bf16[32,16,512]{2,1,0:T(8,128)(2,1)}), bf16[32,16,512]{2,1,0:T(8,128)(2,1)S(1)}, u32[]{:S(2)}, u32[]{:S(2)}) %all-to-all-start.1) | async-done | bytes 524320 | tf_op jit(solution)/shard_map/all_to_all | solution.py:209
  40.9 1.2 gather_fusion.1
  42.5 2.2 %multiply_convert_fusion = (bf16[256,2048]{1,0:T(8,128)(2,1)S(1)}, f32[256,2048]{1,0:T(8,128)}) fusion(bf16[512,2048]{1,0:T(8,128)(2,1)S(1)} %copy-done, f32[256]{0:T(256)S(1)} %fusion.26, f32[256]{0:T(256)S(1)} %broadcast_multiply_fusion.1, bf16[256,512]{1,0:T(8,128)(2,1)S(1)} %gather_fusion.1, pred[256]{0:T(512)(128)(4,1)S(1)} %get-tuple-element.12), kind=kOutput, calls=%fused_computation.15 | convolution fusion | flops 540147712 | bytes 5507328 | tf_op jit(solution)/shard_map/jvp()/dot_general | solution.py:27
  44.7 1.0 copy-done.3
  46.1 2.1 %select_convert_fusion = (bf16[8,256,256]{2,1,0:T(8,128)(2,1)S(1)}, f32[8,256,256]{2,1,0:T(8,128)}) fusion(pred[256,256]{1,0:T(8,128)(4,1)S(1)} %fusion.25, bf16[256,8,64]{0,2,1:T(8,128)(2,1)S(1)} %bitcast.81, bf16[256,8,64]{0,2,1:T(8,128)(2,1)S(1)} %bitcast.79), kind=kOutput, calls=%fused_computation.13 | convolution fusion | flops 70778880 | bytes 3735552 | tf_op jit(solution)/shard_map/jvp(qhd,khd->hqk)/dot_general | solution.py:36
  49.5 1.6 %multiply_reduce_fusion = (f32[256]{0:T(256)S(1)}, f32[256,512]{1,0:T(8,128)S(1)}) fusion(f32[256,512]{1,0:T(8,128)S(1)} %copy.58, f32[256]{0:T(256)S(1)} %broadcast_multiply_fusion, bf16[256,2048]{1,0:T(8,128)(2,1)} %copy-done.3, bf16[512,512]{1,0:T(8,128)(2,1)} %param.12, bf16[1,256,512]{2,1,0:T(8,128)(2,1)} %param.13), kind=kOutput, calls=%fused_computation.51 | convolution fusion | flops 135134976 | bytes 2099200 | tf_op jit(solution)/shard_map/transpose(jvp())/dot_general | solution.py:44
  51.1 2.0 %fusion.34 = (f32[256]{0:T(256)S(1)}, f32[256,512]{1,0:T(8,128)S(1)}, bf16[256,512]{1,0:T(8,128)(2,1)}, bf16[256,512]{1,0:T(8,128)(2,1)S(1)}) fusion(f32[256]{0:T(256)S(1)} %get-tuple-element.19, f32[256,512]{1,0:T(8,128)S(1)} %copy.58, f32[256]{0:T(256)S(1)} %broadcast_multiply_fusion, f32[256]{0:T(256)S(1)} %get-tuple-element.20, ...), kind=kLoop, calls=%fused_computation.96 | loop fusion | flops 1703680 | bytes 2363392 | tf_op jit(solution)/shard_map/transpose(jvp())/reduce_sum | solution.py:18
  53.4 1.5 %fusion.37 = bf16[8,64,256]{2,1,0:T(8,128)(2,1)S(1)} fusion(bf16[8,64,256]{2,1,0:T(8,128)(2,1)S(1)} %bitcast.85, bf16[8,256,256]{2,1,0:T(8,128)(2,1)} %copy-done.1), kind=kOutput, calls=%fused_computation.99 | convolution fusion | flops 67108864 | bytes 1572864 | tf_op jit(solution)/shard_map/transpose(jvp(hqk,khd->qhd))/dot_general | solution.py:40
  54.9 2.9 %fusion.4 = bf16[8,256,256]{2,1,0:T(8,128)(2,1)S(1)} fusion(f32[8,256,256]{2,1,0:T(8,128)} %get-tuple-element.24, bf16[8,64,256]{2,1,0:T(8,128)(2,1)S(1)} %bitcast.86, bf16[256,8,64]{0,2,1:T(8,128)(2,1)S(1)} %bitcast.78, pred[256,256]{1,0:T(8,128)(4,1)S(1)} %fusion.25), kind=kOutput, calls=%fused_computation.12 | convolution fusion | flops 74448896 | bytes 3735552 | tf_op jit(solution)/shard_map/transpose(jvp(hqk,khd->qhd))/dot_general | solution.py:40
  60.4 3.4 %fusion.17 = (f32[256]{0:T(256)S(1)}, f32[256,512]{1,0:T(8,128)S(1)}) fusion(f32[256]{0:T(256)S(1)} %broadcast_multiply_fusion.1, bf16[256,512]{1,0:T(8,128)(2,1)S(1)} %gather_fusion.1, pred[256]{0:T(512)(128)(4,1)S(1)} %get-tuple-element.12, bf16[512,2048]{1,0:T(8,128)(2,1)S(1)} %copy-done, f32[256,2048]{1,0:T(8,128)} %get-tuple-element.22, ...), kind=kOutput, calls=%fused_computation.45 | convolution fusion | flops 546701056 | bytes 6031616 | tf_op jit(solution)/shard_map/transpose(jvp())/dot_general | solution.py:27
  64.4 2.0 %gather_fusion.2 = bf16[512,512]{1,0:T(8,128)(2,1)S(1)} fusion(bf16[256,512]{1,0:T(8,128)(2,1)S(1)} %fusion.21, s32[1024]{0:T(1024)S(1)} %pad_clamp_fusion), kind=kCustom, calls=%fused_computation.2 | custom fusion | bytes 1050624 | tf_op jit(solution)/shard_map/jit(_take)/gather | solution.py:218
  67.4 3.2 %all-to-all-start.2 = ((bf16[32,16,512]{2,1,0:T(8,128)(2,1)}), bf16[32,16,512]{2,1,0:T(8,128)(2,1)S(1)}, u32[]{:S(2)}, u32[]{:S(2)}) async-start(bf16[32,16,512]{2,1,0:T(8,128)(2,1)} %broadcast_select_fusion), calls=%async_computation.2 | async-start | bytes 1048576 | tf_op jit(solution)/shard_map/all_to_all | solution.py:219
  70.9 3.2 %convolution_convert_fusion.in_ref = bf16[512,2048]{1,0:T(8,128)(2,1)S(1)} fusion(f32[256]{0:T(256)S(1)} %fusion.26, f32[256]{0:T(256)S(1)} %broadcast_multiply_fusion.1, bf16[256,512]{1,0:T(8,128)(2,1)S(1)} %gather_fusion.1, pred[256]{0:T(512)(128)(4,1)S(1)} %get-tuple-element.12, f32[256,2048]{1,0:T(8,128)} %get-tuple-element.22, ...), kind=kOutput, calls=%fused_computation.5 | convolution fusion | flops 547487744 | bytes 5507328 | tf_op jit(solution)/shard_map/transpose(jvp())/dot_general | solution.py:27
  74.1 48.1 %shard_map.102 = (bf16[512,2048]{1,0:T(8,128)(2,1)S(1)}, bf16[512,512]{1,0:T(8,128)(2,1)S(1)}) custom-call(bf16[512,2048]{1,0:T(8,128)(2,1)S(1)} %convolution_convert_fusion.in_ref, bf16[512,512]{1,0:T(8,128)(2,1)S(1)} %convolution_convert_fusion.2.out_ref), custom_call_target="tpu_custom_call" | custom-call | flops 1310720 | bytes 104857600 | tf_op jit(solution)/shard_map/pallas_call | solution.py:164
  122.2 1.1 convert_element_type.119
  123.3 2.5 %convert_element_type.118 = f32[512,2048]{1,0:T(8,128)} convert(bf16[512,2048]{1,0:T(8,128)(2,1)S(1)} %get-tuple-element.6) | non-fusion elementwise | flops 1048576 | bytes 6291456 | tf_op jit(solution)/shard_map/convert_element_type | solution.py:185
  125.8 1.0 fusion.9
  126.8 1.3 fusion.5
  (82 shorter events, 10.9 us)
Async XLA Ops:
  0.6 41.9 %copy-start = (bf16[512,2048]{1,0:T(8,128)(2,1)S(1)}, bf16[512,2048]{1,0:T(8,128)(2,1)}, u32[]{:S(2)}) copy-start(bf16[512,2048]{1,0:T(8,128)(2,1)} %param.11) | copy-start | bytes 6291460
  4.0 14.4 %all-to-all-start = ((s32[32,1,16]{2,1,0:T(1,128)}), s32[32,1,16]{2,1,0:T(1,128)S(1)}, u32[]{:S(2)}, u32[]{:S(2)}) async-start(s32[32,1,16]{2,1,0:T(1,128)} %bitcast.2), calls=%async_computation | async-start | bytes 32768 | tf_op jit(solution)/shard_map/all_to_all | solution.py:204
  21.8 3.7 %copy-start.14 = (s32[1,256,1]{1,2,0:T(1,128)S(1)}, s32[1,256,1]{1,2,0:T(1,128)}, u32[]{:S(2)}) copy-start(s32[1,256,1]{1,2,0:T(1,128)} %param.8) | copy-start | bytes 3076
  21.8 3.7 %copy-start.15 = (s32[1,256]{1,0:T(1,128)S(1)}, s32[1,256]{1,0:T(1,128)}, u32[]{:S(2)}) copy-start(s32[1,256]{1,0:T(1,128)} %param.10) | copy-start | bytes 3076
  22.7 18.2 %all-to-all-start.1 = ((bf16[32,16,512]{2,1,0:T(8,128)(2,1)}), bf16[32,16,512]{2,1,0:T(8,128)(2,1)S(1)}, u32[]{:S(2)}, u32[]{:S(2)}) async-start(bf16[32,16,512]{2,1,0:T(8,128)(2,1)} %broadcast_select_fusion.1), calls=%async_computation.1 | async-start | bytes 1048576 | tf_op jit(solution)/shard_map/all_to_all | solution.py:209
  44.7 1.0 copy-start.3
  45.8 2.4 %copy-start.7 = (bf16[256,512]{0,1:T(8,128)(2,1)}, bf16[256,512]{0,1:T(8,128)(2,1)S(1)}, u32[]{:S(2)}) copy-start(bf16[256,512]{0,1:T(8,128)(2,1)S(1)} %copy.57) | copy-start | bytes 786436
  46.0 2.3 %copy-start.9 = (bf16[256,512]{0,1:T(8,128)(2,1)}, bf16[256,512]{0,1:T(8,128)(2,1)S(1)}, u32[]{:S(2)}) copy-start(bf16[256,512]{0,1:T(8,128)(2,1)S(1)} %copy.56) | copy-start | bytes 786436
  46.1 2.2 %copy-start.4 = (bf16[256,512]{0,1:T(8,128)(2,1)}, bf16[256,512]{0,1:T(8,128)(2,1)S(1)}, u32[]{:S(2)}) copy-start(bf16[256,512]{0,1:T(8,128)(2,1)S(1)} %copy.55) | copy-start | bytes 786436
  48.3 1.0 copy-start.1
  51.1 3.8 %copy-start.5 = (bf16[256,512]{0,1:T(8,128)(2,1)S(1)}, bf16[256,512]{0,1:T(8,128)(2,1)}, u32[]{:S(2)}) copy-start(bf16[256,512]{0,1:T(8,128)(2,1)} %copy-done.4) | copy-start | bytes 786436
  53.1 7.3 %copy-start.12 = (bf16[256,512]{1,0:T(8,128)(2,1)}, bf16[256,512]{1,0:T(8,128)(2,1)S(1)}, u32[]{:S(2)}) copy-start(bf16[256,512]{1,0:T(8,128)(2,1)S(1)} %get-tuple-element.15) | copy-start | bytes 786436
  54.9 2.9 %copy-start.8 = (bf16[256,512]{0,1:T(8,128)(2,1)S(1)}, bf16[256,512]{0,1:T(8,128)(2,1)}, u32[]{:S(2)}) copy-start(bf16[256,512]{0,1:T(8,128)(2,1)} %copy-done.7) | copy-start | bytes 786436
  54.9 3.3 %copy-start.10 = (bf16[256,512]{0,1:T(8,128)(2,1)S(1)}, bf16[256,512]{0,1:T(8,128)(2,1)}, u32[]{:S(2)}) copy-start(bf16[256,512]{0,1:T(8,128)(2,1)} %copy-done.9) | copy-start | bytes 786436
  60.4 3.4 %copy-start.13 = (bf16[256,512]{1,0:T(8,128)(2,1)}, bf16[256,512]{1,0:T(8,128)(2,1)S(1)}, u32[]{:S(2)}) copy-start(bf16[256,512]{1,0:T(8,128)(2,1)S(1)} %copy.61) | copy-start | bytes 786436
  60.4 3.7 %copy-start.2 = (bf16[1,256,512]{2,1,0:T(8,128)(2,1)S(1)}, bf16[1,256,512]{2,1,0:T(8,128)(2,1)}, u32[]{:S(2)}) copy-start(bf16[1,256,512]{2,1,0:T(8,128)(2,1)} %param.13) | copy-start | bytes 786436
  66.4 4.1 %copy-start.6 = (bf16[256,512]{1,0:T(8,128)(2,1)S(1)}, bf16[256,512]{1,0:T(8,128)(2,1)}, u32[]{:S(2)}) copy-start(bf16[256,512]{1,0:T(8,128)(2,1)} %get-tuple-element.14) | copy-start | bytes 786436
  67.4 59.5 %all-to-all-start.2 = ((bf16[32,16,512]{2,1,0:T(8,128)(2,1)}), bf16[32,16,512]{2,1,0:T(8,128)(2,1)S(1)}, u32[]{:S(2)}, u32[]{:S(2)}) async-start(bf16[32,16,512]{2,1,0:T(8,128)(2,1)} %broadcast_select_fusion), calls=%async_computation.2 | async-start | bytes 1048576 | tf_op jit(solution)/shard_map/all_to_all | solution.py:219
  123.3 2.5 %copy-start.11 = (bf16[512,512]{1,0:T(8,128)(2,1)S(1)}, bf16[512,512]{1,0:T(8,128)(2,1)}, u32[]{:S(2)}) copy-start(bf16[512,512]{1,0:T(8,128)(2,1)} %param.12) | copy-start | bytes 1572868

commit v4 on v3

--- a/solution.py
+++ b/solution.py
@@ -185,6 +185,13 @@
     return sums[0].astype(jnp.float32), sums[1].astype(jnp.float32)
 
 
+def pick(one_hot, rows, dim):
+    picked = lax.dot_general(
+        one_hot, rows, (((dim,), (0,)), ((), ())), preferred_element_type=jnp.float32
+    )
+    return picked.astype(rows.dtype)
+
+
 def on_device(table, owner, row_in_shard, segment, w_in, w_out, cotangent):
     shards = lax.axis_size("table")
     row_count = owner.shape[1]
@@ -198,16 +205,16 @@
     rank_own = jnp.sum(earlier.astype(jnp.int32), axis=1)
     slot_index = target * capacity + rank_own
     slot_match = slot_index[None, :] == jnp.arange(slot_total)[:, None]
-    source_row = jnp.sum(jnp.where(slot_match, jnp.arange(row_count)[None, :], 0), axis=1)
     request = jnp.sum(jnp.where(slot_match, local_row[None, :] + 1, 0), axis=1) - 1
     request = request.reshape(shards, capacity)
     asked_rows = lax.all_to_all(request, "table", split_axis=0, concat_axis=0, tiled=True)
-    is_valid = asked_rows >= 0
-    found_rows = jnp.take(table, jnp.maximum(asked_rows, 0).reshape(-1), axis=0).reshape(
-        shards, capacity, -1
-    )
+    row_match = (jnp.arange(vocab_rows)[:, None] == asked_rows.reshape(-1)[None, :]).astype(
+        table.dtype
+    )
+    slot_pick = slot_match.astype(table.dtype)
+    found_rows = pick(row_match, table, 0).reshape(shards, capacity, -1)
     returned = lax.all_to_all(found_rows, "table", split_axis=0, concat_axis=0, tiled=True)
-    embedded = jnp.take(returned.reshape(slot_total, -1), slot_index, axis=0)
+    embedded = pick(slot_pick, returned.reshape(slot_total, -1), 0)
     seg_rows = segment[0]
 
     def local_layer(emb_in, weight_in, weight_out):
@@ -215,13 +222,11 @@
 
     layer_rows, pullback = jax.vjp(local_layer, embedded, w_in, w_out)
     d_emb, d_in, d_out = pullback(cotangent[0])
-    sent_grads = jnp.take(d_emb, source_row, axis=0)
+    sent_grads = pick(slot_pick, d_emb, 1)
     arrived = lax.all_to_all(
         sent_grads.reshape(shards, capacity, -1), "table", split_axis=0, concat_axis=0, tiled=True
     )
     flat_grads = arrived.reshape(slot_total, -1)
-    table_ids = jnp.where(is_valid, asked_rows, vocab_rows).reshape(-1)
-    row_match = (table_ids[None, :] == jnp.arange(vocab_rows)[:, None]).astype(flat_grads.dtype)
     partial_sum = jnp.dot(row_match, flat_grads, preferred_element_type=jnp.float32)
     grad_table = lax.psum(partial_sum.astype(jnp.bfloat16), "dp").astype(jnp.float32)
     copies = lax.axis_size("dp")

time: 129 us -> 135 us (1.047)
  blocking collectives: 0 us -> 14.3 us
  starting transfers between devices: 13.1 us -> 6.12 us
  matrix products: 20.7 us -> 27.4 us
  waiting for transfers between devices: 21.1 us -> 15.4 us
  other arithmetic: 12.3 us -> 10.4 us
    all_to_all x0 -> x1, blocking collectives: none -> 14.3 us  [on_device(): lax.all_to_all(request, 'table', split_axis=0, concat_axis=0, tiled=True)]
    all_to_all x1 -> x0, starting transfers between devices: 7.3 us -> none  [on_device(): lax.all_to_all(request, 'table', split_axis=0, concat_axis=0, tiled=True)]
    all_to_all x1 -> x0, waiting for transfers between devices: 7.06 us -> none  [on_device(): lax.all_to_all(request, 'table', split_axis=0, concat_axis=0, tiled=True)]
    gather x3 -> x0, local copies, waits for them, and re-layouts: 6.16 us -> none  [the longest x1 3.04 us: on_device(): jnp.take(table, jnp.maximum(asked_rows, 0).reshape(-1), axis=0)]
    dot_general x0 -> x3, matrix products: none -> 3.92 us  [pick(): lax.dot_general(one_hot, rows, (((dim,), (0,)), ((), ())), preferred_elem...]
    select_n x5 -> x0, other arithmetic: 1.88 us -> none  [the longest x2 0.94 us: on_device(): sent_grads = jnp.take(d_emb, source_row, axis=0)]
    reshape x1, local copies, waits for them, and re-layouts: 0.14 us -> 1.89 us  [hstu_layer(): mixed_all[:, 2 * width:3 * width].reshape(row_count, HEADS, head_size)]
    add_any x1, local copies, waits for them, and re-layouts: 0.13 us -> 1.79 us  [normalize(): average = jnp.mean(values, axis=-1, keepdims=True)]
  transfers between devices with their start and end apart: 3 -> 2, of which waited for: 2 -> 1; matrix products, arithmetic and copies ran while one was open for 7% -> 6% of each run, Pallas kernels for 38% -> 36%
where the time goes in v4:
time: 135 us; the launch traced here: 134 us
  Pallas kernels  47.8 us (35%)
  matrix products  27.4 us (20%)
  waiting for transfers between devices  15.4 us (11%)
  blocking collectives  14.3 us (11%)
  local copies, waits for them, and re-layouts  12.2 us (9%)
  other arithmetic  10.4 us (8%)
  starting transfers between devices  6.12 us (5%)
    pallas_call x1, Pallas kernels, sum_shares(): pl.pallas_call(functools.partial(sum_shares_kernel, shards, parts), out_s...  47.8 us
    all_to_all x1, waiting for transfers between devices, on_device(): lax.all_to_all(found_rows, 'table', split_axis=0, concat_axis=0, tiled=True)  15.4 us
    all_to_all x1, blocking collectives, on_device(): lax.all_to_all(request, 'table', split_axis=0, concat_axis=0, tiled=True)  14.3 us
    dot_general x3, matrix products, hstu_layer(): jnp.dot(normed, w_in, preferred_element_type=jnp.float32)  8.06 us
    dot_general x3, matrix products, hstu_layer(): jnp.einsum('hqk,khd->qhd', weights, value_part, preferred_element_type=jn...  5.74 us
    dot_general x3, matrix products, hstu_layer(): jnp.einsum('qhd,khd->hqk', query_part, key_part, preferred_element_type=j...  4.27 us
    dot_general x3, matrix products, pick(): lax.dot_general(one_hot, rows, (((dim,), (0,)), ((), ())), preferred_elem...  3.92 us
    convert_element_type x2, other arithmetic, sum_shares(): return (sums[0].astype(jnp.float32), sums[1].astype(jnp.float32))  3.64 us
  transfers between devices with their start and end apart: 2, of which 1 were waited for; matrix products, arithmetic and copies ran while one was open for 6% of the time, Pallas kernels for 36%

profile of v4, /device:TPU:0, one launch (start us, length us, event | category | flops | bytes accessed | tf_op | source)
XLA Modules:
  0.0 134.5 jit_solution(4135232609796098757)
XLA Ops:
  0.7 1.0 convert_reduce_fusion
  3.3 14.3 %all_to_all.16 = s32[32,1,16]{2,1,0:T(1,128)S(1)} all-to-all(s32[32,1,16]{2,1,0:T(1,128)S(1)} %bitcast.79), channel_id=1, replica_groups=mesh['table'=32,'dp'=1] {'table'}, dimensions={0} | all-to-all | bytes 4096 | tf_op jit(solution)/shard_map/all_to_all | solution.py:210
  18.8 2.3 %convolution_convert_fusion.4 = bf16[512,512]{1,0:T(8,128)(2,1)} fusion(bf16[384,512]{1,0:T(8,128)(2,1)} %param.7, s32[512]{0:T(512)S(1)} %eq.67), kind=kOutput, calls=%fused_computation.17 | convolution fusion | flops 201785344 | bytes 919552 | tf_op jit(solution)/shard_map/dot_general | solution.py:189
  21.1 2.6 %all-to-all-start.1 = ((bf16[32,16,512]{2,1,0:T(8,128)(2,1)}), bf16[32,16,512]{2,1,0:T(8,128)(2,1)S(1)}, u32[]{:S(2)}, u32[]{:S(2)}) async-start(bf16[32,16,512]{2,1,0:T(8,128)(2,1)} %bitcast.3), calls=%async_computation.1 | async-start | bytes 1048576 | tf_op jit(solution)/shard_map/all_to_all | solution.py:216
  23.8 15.4 %all-to-all-done.1 = bf16[32,16,512]{2,1,0:T(8,128)(2,1)S(1)} async-done(((bf16[32,16,512]{2,1,0:T(8,128)(2,1)}), bf16[32,16,512]{2,1,0:T(8,128)(2,1)S(1)}, u32[]{:S(2)}, u32[]{:S(2)}) %all-to-all-start.1) | async-done | bytes 524320 | tf_op jit(solution)/shard_map/all_to_all | solution.py:216
  39.9 2.1 %multiply_convert_fusion = (bf16[256,2048]{1,0:T(8,128)(2,1)S(1)}, f32[256,2048]{1,0:T(8,128)}) fusion(bf16[512,2048]{1,0:T(8,128)(2,1)S(1)} %copy-done, f32[256,512]{1,0:T(8,128)S(1)} %get-tuple-element.20, f32[256]{0:T(256)S(1)} %fusion.26, f32[256]{0:T(256)S(1)} %broadcast_multiply_fusion.1), kind=kOutput, calls=%fused_computation.12 | convolution fusion | flops 539885568 | bytes 5769216 | tf_op jit(solution)/shard_map/jvp()/dot_general | solution.py:27
  43.9 1.2 copy.41
  46.0 2.1 %select_convert_fusion = (bf16[8,256,256]{2,1,0:T(8,128)(2,1)S(1)}, f32[8,256,256]{2,1,0:T(8,128)}) fusion(pred[256,256]{1,0:T(8,128)(4,1)S(1)} %fusion.25, bf16[256,8,64]{0,2,1:T(8,128)(2,1)S(1)} %bitcast.72, bf16[256,8,64]{0,2,1:T(8,128)(2,1)S(1)} %bitcast.70), kind=kOutput, calls=%fused_computation.10 | convolution fusion | flops 70778880 | bytes 3735552 | tf_op jit(solution)/shard_map/jvp(qhd,khd->hqk)/dot_general | solution.py:36
  50.7 1.8 %multiply_reduce_fusion.1 = (f32[256]{0:T(256)S(1)}, f32[256,512]{1,0:T(8,128)S(1)}) fusion(f32[256,512]{1,0:T(8,128)} %copy.43, f32[256]{0:T(256)S(1)} %broadcast_multiply_fusion, bf16[256,2048]{1,0:T(8,128)(2,1)} %copy-done.5, bf16[512,512]{1,0:T(8,128)(2,1)} %param.12, bf16[1,256,512]{2,1,0:T(8,128)(2,1)S(1)} %copy-done.3), kind=kOutput, calls=%fused_computation.44 | convolution fusion | flops 135134976 | bytes 2099200 | tf_op jit(solution)/shard_map/transpose(jvp())/dot_general | solution.py:44
  52.5 2.0 %fusion.32 = (f32[256]{0:T(256)S(1)}, f32[256,512]{1,0:T(8,128)S(1)}, bf16[256,512]{1,0:T(8,128)(2,1)S(1)}, bf16[256,512]{1,0:T(8,128)(2,1)}) fusion(f32[256]{0:T(256)S(1)} %get-tuple-element.17, f32[256,512]{1,0:T(8,128)S(1)} %copy-done.1, f32[256]{0:T(256)S(1)} %broadcast_multiply_fusion, f32[256]{0:T(256)S(1)} %get-tuple-element.18, ...), kind=kLoop, calls=%fused_computation.79 | loop fusion | flops 1703680 | bytes 2363392 | tf_op jit(solution)/shard_map/transpose(jvp())/reduce_sum | solution.py:18
  55.3 1.8 %copy.44 = bf16[256,512]{0,1:T(8,128)(2,1)} copy(bf16[256,512]{1,0:T(8,128)(2,1)} %broadcast_add_fusion) | data formatting | bytes 524288 | tf_op jit(solution)/shard_map/transpose(jvp())/add_any | solution.py:17
  57.1 2.3 %fusion.36 = bf16[8,64,256]{2,1,0:T(8,128)(2,1)} fusion(bf16[8,64,256]{2,1,0:T(8,128)(2,1)} %bitcast.76, bf16[8,256,256]{2,1,0:T(8,128)(2,1)} %copy-done.2), kind=kOutput, calls=%fused_computation.83 | convolution fusion | flops 67108864 | bytes 1572864 | tf_op jit(solution)/shard_map/transpose(jvp(hqk,khd->qhd))/dot_general | solution.py:40
  59.4 3.0 %fusion.4 = bf16[8,256,256]{2,1,0:T(8,128)(2,1)S(1)} fusion(f32[8,256,256]{2,1,0:T(8,128)} %get-tuple-element.24, bf16[8,64,256]{2,1,0:T(8,128)(2,1)} %bitcast.77, bf16[256,8,64]{0,2,1:T(8,128)(2,1)S(1)} %bitcast.69, pred[256,256]{1,0:T(8,128)(4,1)S(1)} %fusion.25), kind=kOutput, calls=%fused_computation.9 | convolution fusion | flops 74448896 | bytes 3735552 | tf_op jit(solution)/shard_map/transpose(jvp(hqk,khd->qhd))/dot_general | solution.py:40
  62.4 1.1 fusion.37
  65.4 1.1 copy.45
  66.5 1.9 %copy.46 = bf16[256,512]{1,0:T(8,128)(2,1)} copy(bf16[256,512]{0,1:T(8,128)(2,1)} %bitcast.75) | data formatting | bytes 524288 | tf_op jit(solution)/shard_map/transpose(jvp())/reshape | solution.py:32
  68.4 2.9 %multiply_reduce_fusion = (f32[256]{0:T(256)S(1)}, f32[256,512]{1,0:T(8,128)S(1)}) fusion(f32[256,512]{1,0:T(8,128)S(1)} %get-tuple-element.20, f32[256]{0:T(256)S(1)} %broadcast_multiply_fusion.1, bf16[512,2048]{1,0:T(8,128)(2,1)S(1)} %copy-done, f32[256,2048]{1,0:T(8,128)} %get-tuple-element.22, bf16[256,512]{1,0:T(8,128)(2,1)} %get-tuple-element.13, ...), kind=kOutput, calls=%fused_computation.42 | convolution fusion | flops 546438912 | bytes 6293504 | tf_op jit(solution)/shard_map/transpose(jvp())/dot_general | solution.py:27
  71.5 1.2 convolution_convert_fusion.3
  72.7 3.5 %all-to-all-start.2 = ((bf16[32,16,512]{2,1,0:T(8,128)(2,1)}), bf16[32,16,512]{2,1,0:T(8,128)(2,1)}, u32[]{:S(2)}, u32[]{:S(2)}) async-start(bf16[32,16,512]{2,1,0:T(8,128)(2,1)} %bitcast.66), calls=%async_computation.2 | async-start | bytes 1048576 | tf_op jit(solution)/shard_map/all_to_all | solution.py:226
  76.6 3.1 %convolution_convert_fusion.in_ref = bf16[512,2048]{1,0:T(8,128)(2,1)S(1)} fusion(f32[256,512]{1,0:T(8,128)S(1)} %get-tuple-element.20, f32[256]{0:T(256)S(1)} %fusion.26, f32[256]{0:T(256)S(1)} %broadcast_multiply_fusion.1, f32[256,2048]{1,0:T(8,128)} %get-tuple-element.22, bf16[256,512]{1,0:T(8,128)(2,1)S(1)} %copy-done.13, bf16[256,512]{1,0:T(8,128)(2,1)} %copy.47, ...), kind=kOutput, calls=%fused_computation.2 | convolution fusion | flops 547225600 | bytes 5769216 | tf_op jit(solution)/shard_map/transpose(jvp())/dot_general | solution.py:27
  79.7 47.8 %shard_map.102 = (bf16[512,2048]{1,0:T(8,128)(2,1)S(1)}, bf16[512,512]{1,0:T(8,128)(2,1)S(1)}) custom-call(bf16[512,2048]{1,0:T(8,128)(2,1)S(1)} %convolution_convert_fusion.in_ref, bf16[512,512]{1,0:T(8,128)(2,1)S(1)} %convolution_convert_fusion.2.out_ref), custom_call_target="tpu_custom_call" | custom-call | flops 1310720 | bytes 104857600 | tf_op jit(solution)/shard_map/pallas_call | solution.py:164
  127.5 1.1 convert_element_type.132
  128.6 2.5 %convert_element_type.131 = f32[512,2048]{1,0:T(8,128)} convert(bf16[512,2048]{1,0:T(8,128)(2,1)S(1)} %get-tuple-element.6) | non-fusion elementwise | flops 1048576 | bytes 6291456 | tf_op jit(solution)/shard_map/convert_element_type | solution.py:185
  132.2 2.3 %fusion.5 = f32[384,512]{1,0:T(8,128)} fusion(bf16[512,512]{1,0:T(8,128)(2,1)} %bitcast.23, s32[512]{0:T(512)S(1)} %eq.67), kind=kOutput, calls=%fused_computation.19 | convolution fusion | flops 201916416 | bytes 1312768 | tf_op jit(solution)/shard_map/dot_general | solution.py:230
  (63 shorter events, 13.2 us)
Async XLA Ops:
  0.6 39.3 %copy-start = (bf16[512,2048]{1,0:T(8,128)(2,1)S(1)}, bf16[512,2048]{1,0:T(8,128)(2,1)}, u32[]{:S(2)}) copy-start(bf16[512,2048]{1,0:T(8,128)(2,1)} %param.11) | copy-start | bytes 6291460
  0.6 23.1 %copy-start.15 = (s32[1,256]{1,0:T(1,128)S(1)}, s32[1,256]{1,0:T(1,128)}, u32[]{:S(2)}) copy-start(s32[1,256]{1,0:T(1,128)} %param.10) | copy-start | bytes 3076
  21.1 18.2 %all-to-all-start.1 = ((bf16[32,16,512]{2,1,0:T(8,128)(2,1)}), bf16[32,16,512]{2,1,0:T(8,128)(2,1)S(1)}, u32[]{:S(2)}, u32[]{:S(2)}) async-start(bf16[32,16,512]{2,1,0:T(8,128)(2,1)} %bitcast.3), calls=%async_computation.1 | async-start | bytes 1048576 | tf_op jit(solution)/shard_map/all_to_all | solution.py:216
  42.0 1.0 copy-start.5
  43.9 2.0 %copy-start.8 = (bf16[256,512]{0,1:T(8,128)(2,1)}, bf16[256,512]{0,1:T(8,128)(2,1)S(1)}, u32[]{:S(2)}) copy-start(bf16[256,512]{0,1:T(8,128)(2,1)S(1)} %copy.42) | copy-start | bytes 786436
  45.1 3.0 %copy-start.10 = (bf16[256,512]{0,1:T(8,128)(2,1)}, bf16[256,512]{0,1:T(8,128)(2,1)S(1)}, u32[]{:S(2)}) copy-start(bf16[256,512]{0,1:T(8,128)(2,1)S(1)} %copy.41) | copy-start | bytes 786436
  46.0 3.1 %copy-start.6 = (bf16[256,512]{0,1:T(8,128)(2,1)S(1)}, bf16[256,512]{0,1:T(8,128)(2,1)}, u32[]{:S(2)}) copy-start(bf16[256,512]{0,1:T(8,128)(2,1)} %copy.40) | copy-start | bytes 786436
  48.1 1.0 copy-start.2
  48.1 2.6 %copy-start.3 = (bf16[1,256,512]{2,1,0:T(8,128)(2,1)S(1)}, bf16[1,256,512]{2,1,0:T(8,128)(2,1)}, u32[]{:S(2)}) copy-start(bf16[1,256,512]{2,1,0:T(8,128)(2,1)} %param.13) | copy-start | bytes 786436
  50.7 1.8 %copy-start.1 = (f32[256,512]{1,0:T(8,128)S(1)}, f32[256,512]{1,0:T(8,128)}, u32[]{:S(2)}) copy-start(f32[256,512]{1,0:T(8,128)} %copy.43) | copy-start | bytes 1572868
  52.5 6.9 %copy-start.7 = (bf16[256,512]{0,1:T(8,128)(2,1)S(1)}, bf16[256,512]{0,1:T(8,128)(2,1)}, u32[]{:S(2)}) copy-start(bf16[256,512]{0,1:T(8,128)(2,1)} %copy.40) | copy-start | bytes 786436
  59.4 3.0 %copy-start.9 = (bf16[256,512]{0,1:T(8,128)(2,1)S(1)}, bf16[256,512]{0,1:T(8,128)(2,1)}, u32[]{:S(2)}) copy-start(bf16[256,512]{0,1:T(8,128)(2,1)} %copy-done.8) | copy-start | bytes 786436
  59.4 4.1 %copy-start.11 = (bf16[256,512]{0,1:T(8,128)(2,1)S(1)}, bf16[256,512]{0,1:T(8,128)(2,1)}, u32[]{:S(2)}) copy-start(bf16[256,512]{0,1:T(8,128)(2,1)} %copy-done.10) | copy-start | bytes 786436
  62.4 2.1 %copy-start.12 = (bf16[8,64,256]{2,1,0:T(8,128)(2,1)S(1)}, bf16[8,64,256]{2,1,0:T(8,128)(2,1)}, u32[]{:S(2)}) copy-start(bf16[8,64,256]{2,1,0:T(8,128)(2,1)} %fusion.36) | copy-start | bytes 786436
  66.5 4.8 %copy-start.14 = (bf16[256,512]{1,0:T(8,128)(2,1)}, bf16[256,512]{1,0:T(8,128)(2,1)S(1)}, u32[]{:S(2)}) copy-start(bf16[256,512]{1,0:T(8,128)(2,1)S(1)} %copy.45) | copy-start | bytes 786436
  71.5 5.1 %copy-start.13 = (bf16[256,512]{1,0:T(8,128)(2,1)S(1)}, bf16[256,512]{1,0:T(8,128)(2,1)}, u32[]{:S(2)}) copy-start(bf16[256,512]{1,0:T(8,128)(2,1)} %get-tuple-element.13) | copy-start | bytes 786436
  72.7 59.4 %all-to-all-start.2 = ((bf16[32,16,512]{2,1,0:T(8,128)(2,1)}), bf16[32,16,512]{2,1,0:T(8,128)(2,1)}, u32[]{:S(2)}, u32[]{:S(2)}) async-start(bf16[32,16,512]{2,1,0:T(8,128)(2,1)} %bitcast.66), calls=%async_computation.2 | async-start | bytes 1048576 | tf_op jit(solution)/shard_map/all_to_all | solution.py:226
  128.6 2.5 %copy-start.4 = (bf16[512,512]{1,0:T(8,128)(2,1)S(1)}, bf16[512,512]{1,0:T(8,128)(2,1)}, u32[]{:S(2)}) copy-start(bf16[512,512]{1,0:T(8,128)(2,1)} %param.12) | copy-start | bytes 1572868

commit v5 on v4

--- a/solution.py
+++ b/solution.py
@@ -214,7 +214,7 @@
     slot_pick = slot_match.astype(table.dtype)
     found_rows = pick(row_match, table, 0).reshape(shards, capacity, -1)
     returned = lax.all_to_all(found_rows, "table", split_axis=0, concat_axis=0, tiled=True)
-    embedded = pick(slot_pick, returned.reshape(slot_total, -1), 0)
+    embedded = jnp.take(returned.reshape(slot_total, -1), slot_index, axis=0)
     seg_rows = segment[0]
 
     def local_layer(emb_in, weight_in, weight_out):

time: 135 us -> 127 us (0.941)
  local copies, waits for them, and re-layouts: 12.2 us -> 6.54 us
  matrix products: 27.4 us -> 25.7 us
    add_any x1, local copies, waits for them, and re-layouts: 1.79 us -> 0.13 us  [normalize(): average = jnp.mean(values, axis=-1, keepdims=True)]
    dot_general x3 -> x2, matrix products: 3.92 us -> 3.61 us  [pick(): lax.dot_general(one_hot, rows, (((dim,), (0,)), ((), ())), preferred_elem...]
  transfers between devices with their start and end apart: 2 -> 2, of which waited for: 1 -> 1; matrix products, arithmetic and copies ran while one was open for 6% -> 7% of each run, Pallas kernels for 36% -> 38%
where the time goes in v5:
time: 127 us
  Pallas kernels  48.2 us (38%)
  matrix products  25.7 us (20%)
  waiting for transfers between devices  15.4 us (12%)
  blocking collectives  14.3 us (11%)
  other arithmetic  9.96 us (8%)
  local copies, waits for them, and re-layouts  6.54 us (5%)
  starting transfers between devices  5.76 us (5%)
    pallas_call x1, Pallas kernels, sum_shares(): pl.pallas_call(functools.partial(sum_shares_kernel, shards, parts), out_s...  48.2 us
    all_to_all x1, waiting for transfers between devices, on_device(): lax.all_to_all(found_rows, 'table', split_axis=0, concat_axis=0, tiled=True)  15.4 us
    all_to_all x1, blocking collectives, on_device(): lax.all_to_all(request, 'table', split_axis=0, concat_axis=0, tiled=True)  14.3 us
    dot_general x3, matrix products, hstu_layer(): jnp.dot(normed, w_in, preferred_element_type=jnp.float32)  8.7 us
    dot_general x3, matrix products, hstu_layer(): jnp.einsum('hqk,khd->qhd', weights, value_part, preferred_element_type=jn...  5.57 us
    convert_element_type x2, other arithmetic, sum_shares(): return (sums[0].astype(jnp.float32), sums[1].astype(jnp.float32))  3.64 us
    dot_general x2, matrix products, pick(): lax.dot_general(one_hot, rows, (((dim,), (0,)), ((), ())), preferred_elem...  3.61 us
    dot_general x3, matrix products, hstu_layer(): jnp.einsum('qhd,khd->hqk', query_part, key_part, preferred_element_type=j...  3.57 us
  transfers between devices with their start and end apart: 2, of which 1 were waited for; matrix products, arithmetic and copies ran while one was open for 7% of the time, Pallas kernels for 38%

profile of v5, /device:TPU:0, one launch (start us, length us, event | category | flops | bytes accessed | tf_op | source)
XLA Modules:
  0.0 126.7 jit_solution(14781290303575734157)
XLA Ops:
  0.7 1.0 convert_reduce_fusion.1
  3.3 14.3 %all_to_all.16 = s32[32,1,16]{2,1,0:T(1,128)S(1)} all-to-all(s32[32,1,16]{2,1,0:T(1,128)S(1)} %bitcast.85), channel_id=1, replica_groups=mesh['table'=32,'dp'=1] {'table'}, dimensions={0} | all-to-all | bytes 4096 | tf_op jit(solution)/shard_map/all_to_all | solution.py:210
  18.8 2.3 %convolution_convert_fusion.4 = bf16[512,512]{1,0:T(8,128)(2,1)} fusion(bf16[384,512]{1,0:T(8,128)(2,1)} %param.7, s32[512]{0:T(512)S(1)} %eq.67), kind=kOutput, calls=%fused_computation.18 | convolution fusion | flops 201785344 | bytes 919552 | tf_op jit(solution)/shard_map/dot_general | solution.py:189
  21.1 2.6 %all-to-all-start.1 = ((bf16[32,16,512]{2,1,0:T(8,128)(2,1)}), bf16[32,16,512]{2,1,0:T(8,128)(2,1)S(1)}, u32[]{:S(2)}, u32[]{:S(2)}) async-start(bf16[32,16,512]{2,1,0:T(8,128)(2,1)} %bitcast.3), calls=%async_computation.1 | async-start | bytes 1048576 | tf_op jit(solution)/shard_map/all_to_all | solution.py:216
  23.9 15.4 %all-to-all-done.1 = bf16[32,16,512]{2,1,0:T(8,128)(2,1)S(1)} async-done(((bf16[32,16,512]{2,1,0:T(8,128)(2,1)}), bf16[32,16,512]{2,1,0:T(8,128)(2,1)S(1)}, u32[]{:S(2)}, u32[]{:S(2)}) %all-to-all-start.1) | async-done | bytes 524320 | tf_op jit(solution)/shard_map/all_to_all | solution.py:216
  39.3 1.2 gather_fusion
  40.9 2.1 %multiply_convert_fusion = (bf16[256,2048]{1,0:T(8,128)(2,1)S(1)}, f32[256,2048]{1,0:T(8,128)}) fusion(bf16[512,2048]{1,0:T(8,128)(2,1)S(1)} %copy-done, f32[256]{0:T(256)S(1)} %fusion.31, f32[256]{0:T(256)S(1)} %broadcast_multiply_fusion.1, bf16[256,512]{1,0:T(8,128)(2,1)S(1)} %gather_fusion, pred[256]{0:T(512)(128)(4,1)S(1)} %get-tuple-element.10), kind=kOutput, calls=%fused_computation.13 | convolution fusion | flops 540147712 | bytes 5507328 | tf_op jit(solution)/shard_map/jvp()/dot_general | solution.py:27
  43.0 1.0 copy-done.2
  44.5 2.1 %select_convert_fusion = (bf16[8,256,256]{2,1,0:T(8,128)(2,1)S(1)}, f32[8,256,256]{2,1,0:T(8,128)}) fusion(pred[256,256]{1,0:T(8,128)(4,1)S(1)} %fusion.30, bf16[256,8,64]{0,2,1:T(8,128)(2,1)S(1)} %bitcast.77, bf16[256,8,64]{0,2,1:T(8,128)(2,1)S(1)} %bitcast.75), kind=kOutput, calls=%fused_computation.11 | convolution fusion | flops 70778880 | bytes 3735552 | tf_op jit(solution)/shard_map/jvp(qhd,khd->hqk)/dot_general | solution.py:36
  47.9 1.6 %multiply_reduce_fusion = (f32[256]{0:T(256)S(1)}, f32[256,512]{1,0:T(8,128)S(1)}) fusion(f32[256,512]{1,0:T(8,128)S(1)} %copy.43, f32[256]{0:T(256)S(1)} %broadcast_multiply_fusion, bf16[256,2048]{1,0:T(8,128)(2,1)} %copy-done.2, bf16[512,512]{1,0:T(8,128)(2,1)} %param.12, bf16[1,256,512]{2,1,0:T(8,128)(2,1)} %param.13), kind=kOutput, calls=%fused_computation.51 | convolution fusion | flops 135134976 | bytes 2099200 | tf_op jit(solution)/shard_map/transpose(jvp())/dot_general | solution.py:44
  49.5 2.0 %fusion.39 = (f32[256]{0:T(256)S(1)}, f32[256,512]{1,0:T(8,128)S(1)}, bf16[256,512]{1,0:T(8,128)(2,1)S(1)}, bf16[256,512]{1,0:T(8,128)(2,1)}) fusion(f32[256]{0:T(256)S(1)} %get-tuple-element.17, f32[256,512]{1,0:T(8,128)S(1)} %copy.43, f32[256]{0:T(256)S(1)} %broadcast_multiply_fusion, f32[256]{0:T(256)S(1)} %get-tuple-element.18, ...), kind=kLoop, calls=%fused_computation.89 | loop fusion | flops 1703680 | bytes 2363392 | tf_op jit(solution)/shard_map/transpose(jvp())/reduce_sum | solution.py:18
  51.8 2.2 %fusion.42 = bf16[8,64,256]{2,1,0:T(8,128)(2,1)} fusion(bf16[8,64,256]{2,1,0:T(8,128)(2,1)S(1)} %bitcast.81, bf16[8,256,256]{2,1,0:T(8,128)(2,1)} %copy-done.1), kind=kOutput, calls=%fused_computation.92 | convolution fusion | flops 67108864 | bytes 1572864 | tf_op jit(solution)/shard_map/transpose(jvp(hqk,khd->qhd))/dot_general | solution.py:40
  54.0 2.9 %fusion.4 = bf16[8,256,256]{2,1,0:T(8,128)(2,1)S(1)} fusion(f32[8,256,256]{2,1,0:T(8,128)} %get-tuple-element.22, bf16[8,64,256]{2,1,0:T(8,128)(2,1)S(1)} %bitcast.82, bf16[256,8,64]{0,2,1:T(8,128)(2,1)S(1)} %bitcast.74, pred[256,256]{1,0:T(8,128)(4,1)S(1)} %fusion.30), kind=kOutput, calls=%fused_computation.10 | convolution fusion | flops 74448896 | bytes 3735552 | tf_op jit(solution)/shard_map/transpose(jvp(hqk,khd->qhd))/dot_general | solution.py:40
  56.9 1.1 fusion.43
  58.3 0.8 copy.47
  60.9 3.4 %fusion.17 = (f32[256]{0:T(256)S(1)}, f32[256,512]{1,0:T(8,128)S(1)}) fusion(f32[256]{0:T(256)S(1)} %broadcast_multiply_fusion.1, bf16[256,512]{1,0:T(8,128)(2,1)S(1)} %gather_fusion, pred[256]{0:T(512)(128)(4,1)S(1)} %get-tuple-element.10, bf16[512,2048]{1,0:T(8,128)(2,1)S(1)} %copy-done, f32[256,2048]{1,0:T(8,128)} %get-tuple-element.20, ...), kind=kOutput, calls=%fused_computation.45 | convolution fusion | flops 546701056 | bytes 6031616 | tf_op jit(solution)/shard_map/transpose(jvp())/dot_general | solution.py:27
  64.6 1.3 %convolution_convert_fusion.3 = bf16[512,512]{1,0:T(8,128)(2,1)} fusion(bf16[1,256,512]{2,1,0:T(8,128)(2,1)S(1)} %copy-done.5, f32[256]{0:T(256)S(1)} %negate_multiply_fusion, s32[256]{0:T(256)S(1)} %get-tuple-element.11, f32[256,512]{1,0:T(8,128)S(1)} %get-tuple-element.28, f32[256]{0:T(256)S(1)} %multiply_multiply_fusion, f32[256]{0:T(256)S(1)} %fusion.31, ...), kind=kOutput, calls=%fused_computation.17 | convolution fusion | flops 135921664 | bytes 1578240 | tf_op jit(solution)/shard_map/dot_general | solution.py:189
  65.9 3.2 %all-to-all-start.2 = ((bf16[32,16,512]{2,1,0:T(8,128)(2,1)}), bf16[32,16,512]{2,1,0:T(8,128)(2,1)S(1)}, u32[]{:S(2)}, u32[]{:S(2)}) async-start(bf16[32,16,512]{2,1,0:T(8,128)(2,1)} %bitcast.84), calls=%async_computation.2 | async-start | bytes 1048576 | tf_op jit(solution)/shard_map/all_to_all | solution.py:226
  69.4 3.2 %convolution_convert_fusion.in_ref = bf16[512,2048]{1,0:T(8,128)(2,1)S(1)} fusion(f32[256]{0:T(256)S(1)} %fusion.31, f32[256]{0:T(256)S(1)} %broadcast_multiply_fusion.1, bf16[256,512]{1,0:T(8,128)(2,1)S(1)} %gather_fusion, pred[256]{0:T(512)(128)(4,1)S(1)} %get-tuple-element.10, f32[256,2048]{1,0:T(8,128)} %get-tuple-element.20, ...), kind=kOutput, calls=%fused_computation.3 | convolution fusion | flops 547487744 | bytes 5507328 | tf_op jit(solution)/shard_map/transpose(jvp())/dot_general | solution.py:27
  72.6 48.2 %shard_map.102 = (bf16[512,2048]{1,0:T(8,128)(2,1)S(1)}, bf16[512,512]{1,0:T(8,128)(2,1)S(1)}) custom-call(bf16[512,2048]{1,0:T(8,128)(2,1)S(1)} %convolution_convert_fusion.in_ref, bf16[512,512]{1,0:T(8,128)(2,1)S(1)} %convolution_convert_fusion.2.out_ref), custom_call_target="tpu_custom_call" | custom-call | flops 1310720 | bytes 104857600 | tf_op jit(solution)/shard_map/pallas_call | solution.py:164
  120.8 1.1 convert_element_type.128
  121.9 2.5 %convert_element_type.127 = f32[512,2048]{1,0:T(8,128)} convert(bf16[512,2048]{1,0:T(8,128)(2,1)S(1)} %get-tuple-element.6) | non-fusion elementwise | flops 1048576 | bytes 6291456 | tf_op jit(solution)/shard_map/convert_element_type | solution.py:185
  124.4 1.0 fusion.9
  125.4 1.3 fusion.5
  (64 shorter events, 8.0 us)
Async XLA Ops:
  0.6 40.3 %copy-start = (bf16[512,2048]{1,0:T(8,128)(2,1)S(1)}, bf16[512,2048]{1,0:T(8,128)(2,1)}, u32[]{:S(2)}) copy-start(bf16[512,2048]{1,0:T(8,128)(2,1)} %param.11) | copy-start | bytes 6291460
  0.6 23.1 %copy-start.13 = (s32[1,256,1]{1,2,0:T(1,128)S(1)}, s32[1,256,1]{1,2,0:T(1,128)}, u32[]{:S(2)}) copy-start(s32[1,256,1]{1,2,0:T(1,128)} %param.8) | copy-start | bytes 3076
  0.7 23.1 %copy-start.14 = (s32[1,256]{1,0:T(1,128)S(1)}, s32[1,256]{1,0:T(1,128)}, u32[]{:S(2)}) copy-start(s32[1,256]{1,0:T(1,128)} %param.10) | copy-start | bytes 3076
  21.1 18.2 %all-to-all-start.1 = ((bf16[32,16,512]{2,1,0:T(8,128)(2,1)}), bf16[32,16,512]{2,1,0:T(8,128)(2,1)S(1)}, u32[]{:S(2)}, u32[]{:S(2)}) async-start(bf16[32,16,512]{2,1,0:T(8,128)(2,1)} %bitcast.3), calls=%async_computation.1 | async-start | bytes 1048576 | tf_op jit(solution)/shard_map/all_to_all | solution.py:216
  43.0 1.0 copy-start.2
  44.2 2.5 %copy-start.6 = (bf16[256,512]{0,1:T(8,128)(2,1)}, bf16[256,512]{0,1:T(8,128)(2,1)S(1)}, u32[]{:S(2)}) copy-start(bf16[256,512]{0,1:T(8,128)(2,1)S(1)} %copy.42) | copy-start | bytes 786436
  44.4 2.3 %copy-start.8 = (bf16[256,512]{0,1:T(8,128)(2,1)}, bf16[256,512]{0,1:T(8,128)(2,1)S(1)}, u32[]{:S(2)}) copy-start(bf16[256,512]{0,1:T(8,128)(2,1)S(1)} %copy.41) | copy-start | bytes 786436
  44.5 2.2 %copy-start.3 = (bf16[256,512]{0,1:T(8,128)(2,1)}, bf16[256,512]{0,1:T(8,128)(2,1)S(1)}, u32[]{:S(2)}) copy-start(bf16[256,512]{0,1:T(8,128)(2,1)S(1)} %copy.40) | copy-start | bytes 786436
  46.7 1.0 copy-start.1
  49.5 4.5 %copy-start.4 = (bf16[256,512]{0,1:T(8,128)(2,1)S(1)}, bf16[256,512]{0,1:T(8,128)(2,1)}, u32[]{:S(2)}) copy-start(bf16[256,512]{0,1:T(8,128)(2,1)} %copy-done.3) | copy-start | bytes 786436
  54.0 2.9 %copy-start.7 = (bf16[256,512]{0,1:T(8,128)(2,1)S(1)}, bf16[256,512]{0,1:T(8,128)(2,1)}, u32[]{:S(2)}) copy-start(bf16[256,512]{0,1:T(8,128)(2,1)} %copy-done.6) | copy-start | bytes 786436
  54.0 4.0 %copy-start.9 = (bf16[256,512]{0,1:T(8,128)(2,1)S(1)}, bf16[256,512]{0,1:T(8,128)(2,1)}, u32[]{:S(2)}) copy-start(bf16[256,512]{0,1:T(8,128)(2,1)} %copy-done.8) | copy-start | bytes 786436
  56.9 1.5 %copy-start.10 = (bf16[8,64,256]{2,1,0:T(8,128)(2,1)S(1)}, bf16[8,64,256]{2,1,0:T(8,128)(2,1)}, u32[]{:S(2)}) copy-start(bf16[8,64,256]{2,1,0:T(8,128)(2,1)} %fusion.42) | copy-start | bytes 786436
  58.0 2.0 %copy-start.11 = (bf16[8,256,64]{1,2,0:T(8,128)(2,1)S(1)}, bf16[8,256,64]{1,2,0:T(8,128)(2,1)}, u32[]{:S(2)}) copy-start(bf16[8,256,64]{1,2,0:T(8,128)(2,1)} %fusion.43) | copy-start | bytes 786436
  60.9 3.7 %copy-start.5 = (bf16[1,256,512]{2,1,0:T(8,128)(2,1)S(1)}, bf16[1,256,512]{2,1,0:T(8,128)(2,1)}, u32[]{:S(2)}) copy-start(bf16[1,256,512]{2,1,0:T(8,128)(2,1)} %param.13) | copy-start | bytes 786436
  65.9 59.5 %all-to-all-start.2 = ((bf16[32,16,512]{2,1,0:T(8,128)(2,1)}), bf16[32,16,512]{2,1,0:T(8,128)(2,1)S(1)}, u32[]{:S(2)}, u32[]{:S(2)}) async-start(bf16[32,16,512]{2,1,0:T(8,128)(2,1)} %bitcast.84), calls=%async_computation.2 | async-start | bytes 1048576 | tf_op jit(solution)/shard_map/all_to_all | solution.py:226
  121.9 2.5 %copy-start.12 = (bf16[512,512]{1,0:T(8,128)(2,1)S(1)}, bf16[512,512]{1,0:T(8,128)(2,1)}, u32[]{:S(2)}) copy-start(bf16[512,512]{1,0:T(8,128)(2,1)} %param.12) | copy-start | bytes 1572868
